TPU v7x, 32 devices: a whole 2x2x4 slice. The times are simulated.
32 devices in a mesh: groups: 2 (over x), tower: 2 (over core), inner: 8 (over z, y).
Axes of the slice: x: 2, y: 2, z: 4, core: 2. Of those that a mesh axis runs over, the one named last changes fastest.
Arguments:
- ids: int32 [2, 64, 2048, 4], P('tower', 'inner', 'groups'), parts along dimension 2, may hold values from 0 to 16383
- bag_len: int32 [2, 64, 2048], P('tower', 'inner', 'groups'), parts along dimension 2, may hold values from 1 to 4
- slot_of_feature: int32 [2, 64], P('tower'), may hold values from 0 to 63, each once within a row
- tables: bfloat16 [2, 64, 16384, 24], P('tower', 'inner'), may hold values from -3 to 3
- cross_w: bfloat16 [2, 1536, 1536], P('tower'), may hold values from -0.15625 to 0.15625
- cross_b: float32 [2, 1536], P('tower'), may hold values from -3 to 3
- comp_w: bfloat16 [2, 1536, 64], P('tower'), may hold values from -0.15625 to 0.15625
- comp_b: float32 [2, 64], P('tower'), may hold values from -3 to 3
- other_towers: bfloat16 [2048, 896], P(('groups', 'inner')), parts along dimension 0, may hold values from -6 to 6
- expert_w: bfloat16 [8, 1024, 512], P('tower'), may hold values from -0.1875 to 0.1875
- expert_b: float32 [8, 512], P('tower'), may hold values from -3 to 3
- gate_w: bfloat16 [1024, 4, 8], replicated, may hold values from -0.1875 to 0.1875
Outputs:
- task_mix: bfloat16 [2048, 4, 512], P(('groups', 'inner'), None, 'tower'), parts along dimension 0
There are 2 independent parts, one for each index of `groups`. A program takes and returns all parts, laid end to end along the dimension named above; an argument that names none is the same for every part. Nothing has to cross between parts.
Inputs may be any that keep to these rules, and one draw needn't show every extreme that they name: `bag_len`: every bag holds at least one id. `slot_of_feature`: each row is a permutation of the 64 slots.
All inputs are finite; a program needn't handle non-finite values.
Results may differ from a plain program's by a relative error of at most 0.0095.
Values may be sent and summed in bfloat16 or wider, within the bound.
No kernel may reach another device: no remote copies, remote signals or barrier semaphores. Data moves between devices by JAX's collectives and lax.ppermute only.
A program may use at most 128 MiB of HBM per device.

v0:
```python
import jax
import jax.numpy as jnp
from jax import lax
from jax.sharding import PartitionSpec as P


def pool_features(lookup, indices, lengths):
    feature_count = lookup.shape[0]
    vocab_rows = lookup.shape[1]
    embed_width = lookup.shape[2]
    sample_count = indices.shape[1]
    bag_size = indices.shape[2]
    offsets = (jnp.arange(feature_count) * vocab_rows)[:, None, None]
    flat_ids = (indices + offsets).reshape(feature_count * sample_count * bag_size)
    flat_table = lookup.reshape(feature_count * vocab_rows, embed_width)
    gathered = jnp.take(flat_table, flat_ids, axis=0, mode="clip")
    gathered = gathered.reshape(feature_count, sample_count, bag_size, embed_width)
    in_bag = (jnp.arange(bag_size)[None, None, :] < lengths[:, :, None]).astype(jnp.bfloat16)
    summed = jnp.einsum("fsbd,fsb->fsd", gathered, in_bag, preferred_element_type=jnp.float32)
    return summed.astype(jnp.bfloat16)


def on_device(
    ids,
    bag_len,
    slot_of_feature,
    tables,
    cross_w,
    cross_b,
    comp_w,
    comp_b,
    other_towers,
    expert_w,
    expert_b,
    gate_w,
):
    inner_size = lax.axis_size("inner")
    tower_size = lax.axis_size("tower")
    feature_count = tables.shape[1]
    sample_count = ids.shape[2]
    embed_width = tables.shape[3]
    pooled_all = pool_features(tables[0], ids[0], bag_len[0])
    pooled = jnp.transpose(pooled_all, (1, 0, 2)).reshape(sample_count, feature_count * embed_width)
    row_count = sample_count // inner_size
    block_rows = min(row_count, 128)
    block_count = row_count // block_rows
    sendable = pooled.reshape(inner_size, block_count, block_rows, feature_count * embed_width)
    slot_total = slot_of_feature.shape[1]
    onehot = (slot_of_feature[0][:, None] == jnp.arange(slot_total)[None, :]).astype(jnp.bfloat16)
    received = lax.all_to_all(sendable, "inner", split_axis=0, concat_axis=3, tiled=True)
    item_count = received.shape[1]
    full_width = received.shape[3]
    features = received.reshape(item_count * block_rows, slot_total, full_width // slot_total)
    first_layer = jnp.einsum("rfd,fg->rgd", features, onehot, preferred_element_type=jnp.float32)
    first_layer = first_layer.astype(jnp.bfloat16).reshape(item_count * block_rows, full_width)
    crossed = jnp.dot(first_layer, cross_w[0], preferred_element_type=jnp.float32) + cross_b[0]
    base = first_layer.astype(jnp.float32)
    next_layer = (base * crossed + base).astype(jnp.bfloat16)
    squeezed = jnp.dot(next_layer, comp_w[0], preferred_element_type=jnp.float32) + comp_b[0]
    compressed = squeezed.astype(jnp.bfloat16).reshape(item_count, block_rows, squeezed.shape[1])
    compressed = compressed.reshape(row_count, compressed.shape[2])
    gathered = lax.all_gather(compressed, "tower", axis=1, tiled=True)
    expert_in = jnp.concatenate([other_towers, gathered], axis=1)
    logits = jnp.einsum("ri,ike->rke", expert_in, gate_w, preferred_element_type=jnp.float32)
    weights = jnp.exp(logits)
    gate_probs = weights / jnp.sum(weights, axis=2, keepdims=True)
    hidden = jnp.einsum("ri,eih->erh", expert_in, expert_w, preferred_element_type=jnp.float32)
    hidden = jnp.maximum(hidden + expert_b[:, None, :], 0.0).astype(jnp.bfloat16)
    exp_local = expert_w.shape[0]
    task_count = gate_w.shape[1]
    hidden_width = hidden.shape[2]
    halves = hidden.reshape(exp_local, row_count, tower_size, hidden_width // tower_size)
    received_all = lax.all_to_all(halves, "tower", split_axis=2, concat_axis=0, tiled=True)
    running = jnp.zeros((row_count, task_count, hidden_width // tower_size), jnp.float32)
    for member in range(exp_local * tower_size):
        running = (
            running
            + gate_probs[:, :, member, None]
            * received_all[member, :, 0, :].astype(jnp.float32)[:, None, :]
        )
    task_mix = running.astype(jnp.bfloat16)
    return task_mix


def solution(mesh):
    return jax.shard_map(
        on_device,
        mesh=mesh,
        in_specs=(
            P("tower", "inner", "groups", None),
            P("tower", "inner", "groups"),
            P("tower", None),
            P("tower", "inner", None, None),
            P("tower", None, None),
            P("tower", None),
            P("tower", None, None),
            P("tower", None),
            P(("groups", "inner"), None),
            P("tower", None, None),
            P("tower", None),
            P(),
        ),
        out_specs=P(("groups", "inner"), None, "tower"),
        check_vma=False,
    )
```

profile of v0, /device:TPU:0, one launch (start us, length us, event | category | flops | bytes accessed | tf_op | source)
XLA Modules:
  0.0 632.7 jit_solution(350731891534048785)
XLA Ops:
  0.0 0.0 copy-start
  0.0 24.4 %copy.54 = bf16[1,8,16384,24]{3,2,1,0:T(8,128)(2,1)} copy(bf16[1,8,16384,24]{2,3,1,0:T(8,128)(2,1)} %param.15) | data formatting | bytes 12582912 | tf_op args[3]
  24.4 2.4 add.70
  26.8 6.1 add.71
  32.9 0.0 copy-done.2
  32.9 0.0 copy-start.3
  32.9 2.7 copy.55
  35.6 6.1 squeeze.6
  41.7 0.1 add.72
  41.9 2.6 copy.77
  44.6 502.2 %gather_fusion = bf16[32768,24]{1,0:T(8,128)(2,1)} fusion(bf16[131072,24]{1,0:T(8,128)(2,1)} %bitcast.123, s32[32768]{0:T(1024)S(1)} %broadcast_clamp_fusion), kind=kCustom, calls=%fused_computation | custom fusion | bytes 3276800 | tf_op jit(solution)/shard_map/jit(_take)/gather | solution.py:16
  546.7 46.9 %multiply_reduce_fusion = bf16[1024,8,24]{2,0,1:T(8,128)(2,1)S(1)} fusion(bf16[1024,8,4,24]{3,2,0,1:T(4,128)(2,1)} %bitcast.124, f32[1024,8,4]{2,0,1:T(8,128)} %copy.77), kind=kLoop, calls=%fused_computation.1 | loop fusion | flops 2162688 | bytes 2097152
  593.7 0.0 copy-start.5
  593.7 0.0 copy-start.7
  593.7 0.0 copy-start.6
  593.7 0.8 copy.76
  594.5 0.1 copy.79
  594.6 0.0 copy-start.1
  594.6 0.0 copy-start.8
  594.6 0.8 copy.56
  595.4 7.8 %all-to-all-start = ((bf16[8,1,128,192]{2,3,1,0:T(8,128)(2,1)}), bf16[8,1,128,192]{2,3,1,0:T(8,128)(2,1)S(1)}, u32[]{:S(2)}, u32[]{:S(2)}) async-start(bf16[8,1,128,192]{2,3,1,0:T(8,128)(2,1)} %copy.56), calls=%async_computation | async-start | bytes 786432 | tf_op jit(solution)/shard_map/all_to_all | solution.py:50
  603.2 0.0 copy-done.5
  603.2 0.0 copy-start.4
  603.2 12.8 %all-to-all-done = bf16[8,1,128,192]{2,3,1,0:T(8,128)(2,1)S(1)} async-done(((bf16[8,1,128,192]{2,3,1,0:T(8,128)(2,1)}), bf16[8,1,128,192]{2,3,1,0:T(8,128)(2,1)S(1)}, u32[]{:S(2)}, u32[]{:S(2)}) %all-to-all-start) | async-done | bytes 393248 | tf_op jit(solution)/shard_map/all_to_all | solution.py:50
  616.0 0.0 copy-done.7
  616.0 0.2 fusion.16
  616.2 0.3 copy.58
  616.5 0.2 copy.59
  616.7 0.0 copy-done
  616.7 0.0 copy-done.6
  616.7 3.3 fusion.23
  620.1 1.8 all_gather.3
  621.9 0.1 copy.60
  622.0 0.0 copy-done.1
  622.0 0.0 copy-done.8
  622.0 0.2 fusion.49
  622.3 0.1 copy.61
  622.4 0.1 copy.63
  622.5 0.1 copy.64
  622.6 0.1 copy.65
  622.7 0.1 copy.66
  622.8 0.1 copy.67
  623.0 0.1 copy.68
  623.1 0.1 copy.69
  623.2 2.9 fusion.15
  626.1 4.2 all_to_all.33
  630.3 0.1 fusion.41
  630.4 2.3 add_convert_fusion
  (10 shorter events, 0.1 us)
Async XLA Ops:
  0.0 616.7 %copy-start = (bf16[1,1536,64]{1,2,0:T(8,128)(2,1)S(1)}, bf16[1,1536,64]{1,2,0:T(8,128)(2,1)}, u32[]{:S(2)}) copy-start(bf16[1,1536,64]{1,2,0:T(8,128)(2,1)} %param.18) | copy-start | bytes 589828
  24.4 8.5 %copy-start.2 = (s32[1,8,1024,4]{2,3,1,0:T(4,128)S(1)}, s32[1,8,1024,4]{2,3,1,0:T(4,128)}, u32[]{:S(2)}) copy-start(s32[1,8,1024,4]{2,3,1,0:T(4,128)} %param.12) | copy-start | bytes 393220
  32.9 9.0 %copy-start.3 = (s32[1,8,1024]{2,1,0:T(8,128)S(1)}, s32[1,8,1024]{2,1,0:T(8,128)}, u32[]{:S(2)}) copy-start(s32[1,8,1024]{2,1,0:T(8,128)} %param.13) | copy-start | bytes 98308
  593.7 9.5 %copy-start.5 = (f32[1,1536]{1,0:T(1,128)S(1)}, f32[1,1536]{1,0:T(1,128)}, u32[]{:S(2)}) copy-start(f32[1,1536]{1,0:T(1,128)} %param.17) | copy-start | bytes 18436
  593.7 22.3 %copy-start.7 = (s32[1,64]{1,0:T(1,128)S(1)}, s32[1,64]{1,0:T(1,128)}, u32[]{:S(2)}) copy-start(s32[1,64]{1,0:T(1,128)} %param.14) | copy-start | bytes 772
  593.7 23.0 %copy-start.6 = (f32[1,64]{1,0:T(1,128)S(1)}, f32[1,64]{1,0:T(1,128)}, u32[]{:S(2)}) copy-start(f32[1,64]{1,0:T(1,128)} %param.19) | copy-start | bytes 772
  594.6 27.4 %copy-start.1 = (bf16[128,896]{1,0:T(8,128)(2,1)S(1)}, bf16[128,896]{1,0:T(8,128)(2,1)}, u32[]{:S(2)}) copy-start(bf16[128,896]{1,0:T(8,128)(2,1)} %param.20) | copy-start | bytes 688132
  594.6 27.4 %copy-start.8 = (bf16[1024,4,8]{0,2,1:T(8,128)(2,1)S(1)}, bf16[1024,4,8]{0,2,1:T(8,128)(2,1)}, u32[]{:S(2)}) copy-start(bf16[1024,4,8]{0,2,1:T(8,128)(2,1)} %param.23) | copy-start | bytes 196612
  595.4 20.6 %all-to-all-start = ((bf16[8,1,128,192]{2,3,1,0:T(8,128)(2,1)}), bf16[8,1,128,192]{2,3,1,0:T(8,128)(2,1)S(1)}, u32[]{:S(2)}, u32[]{:S(2)}) async-start(bf16[8,1,128,192]{2,3,1,0:T(8,128)(2,1)} %copy.56), calls=%async_computation | async-start | bytes 786432 | tf_op jit(solution)/shard_map/all_to_all | solution.py:50
  603.2 20.0 %copy-start.4 = (f32[4,512]{1,0:T(4,128)S(1)}, f32[4,512]{1,0:T(4,128)}, u32[]{:S(2)}) copy-start(f32[4,512]{1,0:T(4,128)} %param.22) | copy-start | bytes 24580
where the time goes:
time: 636 us; the launch traced here: 633 us
  local copies, waits for them, and re-layouts  550 us (86%)
  other arithmetic  49.6 us (8%)
  waiting for transfers between devices  12.8 us (2%)
  starting transfers between devices  7.76 us (1%)
  matrix products  6.71 us (1%)
    gather x1, local copies, waits for them, and re-layouts, pool_features(): gathered = jnp.take(flat_table, flat_ids, axis=0, mode='clip')  502 us
    unnamed x3, other arithmetic  47 us
    unnamed x22, local copies, waits for them, and re-layouts  29.9 us
    all_to_all x1, waiting for transfers between devices, on_device(): lax.all_to_all(sendable, 'inner', split_axis=0, concat_axis=3, tiled=True)  12.8 us
  transfers between devices with their start and end apart: 1, of which 1 were waited for; matrix products, arithmetic and copies ran while one was open for 0% of the time, Pallas kernels for 0%

commit v1 on v0

v1 whole, which is shorter than its diff:
```python
import functools

import jax
import jax.numpy as jnp
from jax import lax
from jax.experimental import pallas as pl
from jax.experimental.pallas import tpu as pltpu
from jax.sharding import PartitionSpec as P

LOW = 256


def gather_kernel(low, tile, ids_ref, len_ref, tab_ref, out_ref, rows_ref):
    feature = pl.program_id(0)
    embed, vocab = tab_ref.shape[1], tab_ref.shape[2]
    bag, samples = ids_ref.shape[1], ids_ref.shape[2]
    row_count = out_ref.shape[3]
    high = vocab // low
    for part in range(0, high, 2):
        pair = [tab_ref[0, :, pl.ds((part + n) * low, low)].astype(jnp.float32) for n in range(2)]
        rows_ref[pl.ds(part * embed, 2 * embed), :] = jnp.concatenate(pair, axis=0).astype(jnp.bfloat16)
    level = lax.broadcasted_iota(jnp.int32, (low, tile), 0)

    def one_tile(step, carry):
        start = pl.multiple_of(step * tile, tile)
        length = len_ref[pl.ds(feature, 1), pl.ds(start, tile)]
        total = jnp.zeros((embed, tile), jnp.float32)
        for slot in range(bag):
            index = ids_ref[feature, pl.ds(slot, 1), pl.ds(start, tile)]
            upper = jnp.where(slot < length, index // low, -1)
            chosen = (level == index % low).astype(jnp.float32).astype(jnp.bfloat16)
            found = jnp.dot(rows_ref[...], chosen, preferred_element_type=jnp.float32)
            picked = jnp.zeros((embed, tile), jnp.float32)
            for part in range(high):
                picked = jnp.where(upper == part, found[part * embed : (part + 1) * embed], picked)
            total = total + picked
        for block in range(tile // row_count):
            piece = total[:, block * row_count : (block + 1) * row_count]
            out_ref[step * (tile // row_count) + block, feature] = piece.astype(jnp.bfloat16)
        return carry

    lax.fori_loop(0, samples // tile, one_tile, 0)


def pool_features(table, ids, lengths, inner_size):
    features, embed, vocab = table.shape
    bag, samples = ids.shape[1], ids.shape[2]
    row_count = samples // inner_size
    tile = row_count * max(1, 512 // row_count)
    whole = lambda shape: pl.BlockSpec(shape, lambda f: (0,) * len(shape))
    out_shape = (inner_size, features, embed, row_count)
    return pl.pallas_call(
        functools.partial(gather_kernel, LOW, tile),
        out_shape=jax.ShapeDtypeStruct(out_shape, jnp.bfloat16),
        grid=(features,),
        in_specs=[
            whole(ids.shape),
            whole(lengths.shape),
            pl.BlockSpec((1, embed, vocab), lambda f: (f, 0, 0)),
        ],
        out_specs=whole(out_shape),
        scratch_shapes=[pltpu.VMEM((vocab // LOW * embed, LOW), jnp.bfloat16)],
        compiler_params=pltpu.CompilerParams(vmem_limit_bytes=40 * 2**20),
        name="pool_features",
    )(ids, lengths, table)


def cross_kernel(blocks, slot_ref, rec_ref, w_hbm, bias_ref, comp_ref, comp_bias_ref, out_ref, first_t, first, w_ref, sems):
    slots, embed, rows = rec_ref.shape
    width = w_ref.shape[1]
    step = width // blocks
    copies = []
    for n in range(blocks):
        span = pl.ds(n * step, step)
        copies.append(pltpu.make_async_copy(w_hbm.at[:, span], w_ref.at[:, span], sems.at[n]))
        copies[-1].start()
    for f in range(slots):
        first_t[slot_ref[f]] = rec_ref[f].astype(jnp.float32)
    first[...] = first_t[...].reshape(width, rows).T.astype(jnp.bfloat16)
    total = jnp.zeros((rows, comp_ref.shape[0]), jnp.float32) + comp_bias_ref[...]
    for n in range(blocks):
        span = pl.ds(n * step, step)
        copies[n].wait()
        crossed = jnp.dot(first[...], w_ref[:, span], preferred_element_type=jnp.float32) + bias_ref[:, span]
        base = first[:, span].astype(jnp.float32)
        second = (base * crossed + base).astype(jnp.bfloat16)
        total = total + lax.dot_general(
            second, comp_ref[:, span], (((1,), (1,)), ((), ())), preferred_element_type=jnp.float32
        )
    out_ref[...] = total.astype(jnp.bfloat16)


def cross_and_compress(received, slots, cross_w, cross_b, comp_w, comp_b):
    slot_total, embed, rows = received.shape
    width = cross_w.shape[0]
    blocks = width // 256
    vmem = pl.BlockSpec(memory_space=pltpu.VMEM)
    return pl.pallas_call(
        functools.partial(cross_kernel, blocks),
        out_shape=jax.ShapeDtypeStruct((rows, comp_w.shape[1]), jnp.bfloat16),
        in_specs=[pl.BlockSpec(memory_space=pltpu.SMEM), vmem, pl.BlockSpec(memory_space=pl.ANY), vmem, vmem, vmem],
        out_specs=vmem,
        scratch_shapes=[
            pltpu.VMEM((slot_total, embed, rows), jnp.float32),
            pltpu.VMEM((rows, width), jnp.bfloat16),
            pltpu.VMEM((width, width), jnp.bfloat16),
            pltpu.SemaphoreType.DMA((blocks,)),
        ],
        compiler_params=pltpu.CompilerParams(vmem_limit_bytes=16 * 2**20),
        name="cross_and_compress",
    )(slots, received, cross_w, cross_b, comp_w.T, comp_b)


def mix_kernel(tower_ref, early_ref, late_w_ref, bias_ref, gate_early_ref, gate_late_ref, own_ref, other_ref, out_ref):
    experts, rows, columns = early_ref.shape
    tasks = gate_early_ref.shape[1] // experts
    mine, other = own_ref[...], other_ref[...]
    lead = tower_ref[0] == 0
    squeezed = jnp.concatenate([jnp.where(lead, mine, other), jnp.where(lead, other, mine)], axis=1)
    logits = gate_early_ref[...] + jnp.dot(squeezed, gate_late_ref[...], preferred_element_type=jnp.float32)
    weights = jnp.exp(logits)
    norm = sum(weights[:, e * tasks : (e + 1) * tasks] for e in range(experts))
    probs = [weights[:, e * tasks : (e + 1) * tasks] / norm for e in range(experts)]
    totals = [jnp.zeros((rows, columns), jnp.float32) for _ in range(tasks)]
    for e in range(experts):
        hidden = early_ref[e] + jnp.dot(squeezed, late_w_ref[e], preferred_element_type=jnp.float32)
        hidden = jnp.maximum(hidden + bias_ref[pl.ds(e, 1), :], 0.0).astype(jnp.bfloat16).astype(jnp.float32)
        for k in range(tasks):
            totals[k] = totals[k] + probs[e][:, k : k + 1] * hidden
    for k in range(tasks):
        out_ref[:, pl.ds(k * columns, columns)] = totals[k].astype(jnp.bfloat16)


def mix_experts(tower, early, late_w, bias, gate_early, gate_late, own, other):
    experts, rows, columns = early.shape
    tasks = gate_early.shape[1] // experts
    vmem = pl.BlockSpec(memory_space=pltpu.VMEM)
    out = pl.pallas_call(
        mix_kernel,
        out_shape=jax.ShapeDtypeStruct((rows, tasks * columns), jnp.bfloat16),
        in_specs=[pl.BlockSpec(memory_space=pltpu.SMEM)] + [vmem] * 7,
        out_specs=vmem,
        compiler_params=pltpu.CompilerParams(vmem_limit_bytes=16 * 2**20),
        name="mix_experts",
    )(tower, early, late_w, bias, gate_early, gate_late, own, other)
    return out.reshape(rows, tasks, columns)


def on_device(
    ids,
    bag_len,
    slot_of_feature,
    tables,
    cross_w,
    cross_b,
    comp_w,
    comp_b,
    other_towers,
    expert_w,
    expert_b,
    gate_w,
):
    inner_size = lax.axis_size("inner")
    tower_size = lax.axis_size("tower")
    tower = lax.axis_index("tower")
    swap = [(n, (n + 1) % tower_size) for n in range(tower_size)]

    far_w = lax.ppermute(expert_w, "tower", swap)
    far_b = lax.ppermute(expert_b, "tower", swap)

    pooled = pool_features(
        jnp.transpose(tables[0], (0, 2, 1)), jnp.transpose(ids[0], (0, 2, 1)), bag_len[0], inner_size
    )
    received = lax.all_to_all(pooled, "inner", split_axis=0, concat_axis=0, tiled=True)
    received = received.reshape((-1,) + received.shape[2:])

    exp_local, expert_in, hidden_width = expert_w.shape
    columns = hidden_width // tower_size
    known = other_towers.shape[1]
    half = lambda x: lax.dynamic_slice_in_dim(x, tower * columns, columns, axis=x.ndim - 1)
    both_w = jnp.concatenate([half(expert_w), half(far_w)], axis=0)
    both_b = jnp.concatenate([half(expert_b), half(far_b)], axis=0)
    early = jnp.einsum("ri,eih->erh", other_towers, both_w[:, :known], preferred_element_type=jnp.float32)
    task_count, expert_count = gate_w.shape[1:]
    gates = jnp.roll(jnp.transpose(gate_w, (2, 1, 0)), -tower * exp_local, axis=0)
    gates = gates.reshape(expert_count * task_count, expert_in)
    gate_early = lax.dot_general(
        other_towers, gates[:, :known], (((1,), (1,)), ((), ())), preferred_element_type=jnp.float32
    )
    gate_late = gates[:, known:].T

    squeezed = cross_and_compress(received, slot_of_feature[0], cross_w[0], cross_b, comp_w[0], comp_b)
    opposite = lax.ppermute(squeezed, "tower", swap)
    return mix_experts(
        tower.reshape(1), early, both_w[:, known:], both_b, gate_early, gate_late, squeezed, opposite
    )


def solution(mesh):
    return jax.shard_map(
        on_device,
        mesh=mesh,
        in_specs=(
            P("tower", "inner", "groups", None),
            P("tower", "inner", "groups"),
            P("tower", None),
            P("tower", "inner", None, None),
            P("tower", None, None),
            P("tower", None),
            P("tower", None, None),
            P("tower", None),
            P(("groups", "inner"), None),
            P("tower", None, None),
            P("tower", None),
            P(),
        ),
        out_specs=P(("groups", "inner"), None, "tower"),
        check_vma=False,
    )
```

time: 636 us -> 66 us (0.10)
  local copies, waits for them, and re-layouts: 550 us -> 11.4 us
  other arithmetic: 49.6 us -> 0.11 us
  Pallas kernels: 0 us -> 35.1 us
    gather x1 -> x0, local copies, waits for them, and re-layouts: 502 us -> none  [pool_features(): gathered = jnp.take(flat_table, flat_ids, axis=0, mode='clip')]
    unnamed x3 -> x0, other arithmetic: 47 us -> none
    pallas_call x0 -> x3, Pallas kernels: none -> 35.1 us  [the longest x1 30.3 us: pool_features(): pl.pallas_call(functools.partial(gather_kernel, LOW, tile), out_shape=jax...]
    unnamed x22 -> x23, local copies, waits for them, and re-layouts: 29.9 us -> 6.93 us
    add x2 -> x0, local copies, waits for them, and re-layouts: 8.48 us -> none  [pool_features(): indices + offsets]
  transfers between devices with their start and end apart: 1 -> 4, of which waited for: 1 -> 1; matrix products, arithmetic and copies ran while one was open for 0% -> 8% of each run, Pallas kernels for 0% -> 52%
where the time goes in v1:
time: 66 us; the launch traced here: 65.5 us
  Pallas kernels  35.1 us (53%)
  local copies, waits for them, and re-layouts  11.4 us (17%)
  waiting for transfers between devices  9.6 us (15%)
  starting transfers between devices  8.01 us (12%)
  matrix products  1.15 us (2%)
    pallas_call x1, Pallas kernels, pool_features(): pl.pallas_call(functools.partial(gather_kernel, LOW, tile), out_shape=jax...  30.3 us
    all_to_all x1, waiting for transfers between devices, on_device(): lax.all_to_all(pooled, 'inner', split_axis=0, concat_axis=0, tiled=True)  9.59 us
    all_to_all x1, starting transfers between devices, on_device(): lax.all_to_all(pooled, 'inner', split_axis=0, concat_axis=0, tiled=True)  7.41 us
    unnamed x23, local copies, waits for them, and re-layouts  6.93 us
    pallas_call x1, Pallas kernels, cross_and_compress(): pl.pallas_call(functools.partial(cross_kernel, blocks), out_shape=jax.Sha...  3.5 us
    dynamic_slice x4, local copies, waits for them, and re-layouts, on_device(): lax.dynamic_slice_in_dim(x, tower * columns, columns, axis=x.ndim - 1)  3.49 us
  transfers between devices with their start and end apart: 4, of which 1 were waited for; matrix products, arithmetic and copies ran while one was open for 8% of the time, Pallas kernels for 52%

profile of v1, /device:TPU:0, one launch (start us, length us, event | category | flops | bytes accessed | tf_op | source)
XLA Modules:
  0.0 65.5 jit_solution(11610684875330059991)
XLA Ops:
  0.0 0.0 copy-start
  0.0 0.5 collective-permute-start
  0.5 0.1 collective-permute-start.1
  0.5 0.0 copy-start.1
  0.5 2.8 %copy-done.1 = bf16[1,8,16384,24]{2,3,1,0:T(8,128)(2,1)S(1)} copy-done((bf16[1,8,16384,24]{2,3,1,0:T(8,128)(2,1)S(1)}, bf16[1,8,16384,24]{2,3,1,0:T(8,128)(2,1)}, u32[]{:S(2)}) %copy-start.1) | copy-done | bytes 6291480
  3.3 0.0 copy-start.4
  3.3 0.9 %copy-done.4 = s32[1,8,1024,4]{2,3,1,0:T(4,128)S(1)} copy-done((s32[1,8,1024,4]{2,3,1,0:T(4,128)S(1)}, s32[1,8,1024,4]{2,3,1,0:T(4,128)}, u32[]{:S(2)}) %copy-start.4) | copy-done | bytes 131096
  4.2 0.0 copy-start.5
  4.2 0.8 %copy-done.5 = s32[1,8,1024]{2,1,0:T(8,128)S(1)} copy-done((s32[1,8,1024]{2,1,0:T(8,128)S(1)}, s32[1,8,1024]{2,1,0:T(8,128)}, u32[]{:S(2)}) %copy-start.5) | copy-done | bytes 32792
  5.0 0.0 copy-start.9
  5.0 30.3 %pool_features.1 = bf16[8,8,24,128]{3,2,1,0:T(8,128)(2,1)} custom-call(s32[8,4,1024]{2,1,0:T(4,128)S(1)} %bitcast.29, s32[8,1024]{1,0:T(8,128)S(1)} %bitcast.30, bf16[8,24,16384]{2,1,0:T(8,128)(2,1)S(1)} %bitcast.24), custom_call_target="tpu_custom_call" | custom-call | tf_op jit(solution)/shard_map/pool_features/pallas_call | solution.py:52
  35.3 0.0 copy-start.10
  35.3 0.0 copy-start.3
  35.3 0.0 copy-start.6
  35.3 0.0 copy-start.7
  35.3 0.0 copy-start.8
  35.3 7.4 %all-to-all-start = ((bf16[8,8,24,128]{3,2,1,0:T(8,128)(2,1)}), bf16[8,8,24,128]{3,2,1,0:T(8,128)(2,1)S(1)}, u32[]{:S(2)}, u32[]{:S(2)}) async-start(bf16[8,8,24,128]{3,2,1,0:T(8,128)(2,1)} %pool_features.1), calls=%async_computation | async-start | bytes 786432 | tf_op jit(solution)/shard_map/all_to_all | solution.py:174
  42.7 0.0 copy-done.9
  42.7 0.1 fusion.7
  42.8 0.1 copy.19
  42.9 1.7 %constant_dynamic-slice_fusion.3 = bf16[4,1024,256]{2,1,0:T(8,128)(2,1)S(1)} fusion(bf16[4,1024,512]{2,1,0:T(8,128)(2,1)} %param.21, s32[]{:T(128)S(6)} %select_n.19), kind=kLoop, calls=%fused_computation.16 | loop fusion | bytes 4194308 | tf_op jit(solution)/shard_map/dynamic_slice | solution.py:180
  44.6 0.0 copy-done
  44.6 0.2 convolution_bitcast_fusion.gate_early_ref
  44.8 0.0 copy-done.10
  44.9 0.1 copy.25
  45.0 0.0 collective-permute-done.1
  45.0 9.6 %all-to-all-done = bf16[8,8,24,128]{3,2,1,0:T(8,128)(2,1)S(1)} async-done(((bf16[8,8,24,128]{3,2,1,0:T(8,128)(2,1)}), bf16[8,8,24,128]{3,2,1,0:T(8,128)(2,1)S(1)}, u32[]{:S(2)}, u32[]{:S(2)}) %all-to-all-start) | async-done | bytes 393248 | tf_op jit(solution)/shard_map/all_to_all | solution.py:174
  54.6 0.0 copy-done.3
  54.6 0.0 copy-done.6
  54.6 0.0 copy-done.7
  54.7 0.0 copy-done.8
  54.7 0.0 copy-start.2
  54.7 2.3 %copy-done.2 = bf16[1,1536,1536]{2,1,0:T(8,128)(2,1)S(1)} copy-done((bf16[1,1536,1536]{2,1,0:T(8,128)(2,1)S(1)}, bf16[1,1536,1536]{2,1,0:T(8,128)(2,1)}, u32[]{:S(2)}) %copy-start.2) | copy-done | bytes 4718616
  57.0 3.5 %cross_and_compress.1.own_ref = bf16[128,64]{1,0:T(8,128)(2,1)S(1)} custom-call(s32[64]{0:T(128)S(1)} %bitcast.31, bf16[64,24,128]{2,1,0:T(8,128)(2,1)S(1)} %bitcast.26, bf16[1536,1536]{1,0:T(8,128)(2,1)S(1)} %bitcast.25, f32[1,1536]{1,0:T(1,128)S(1)} %copy-done.6, bf16[64,1536]{1,0:T(8,128)(2,1)S(1)} %bitcast.27, f32[1,64]{1,0:T(1,128)S(1)} %copy-done.8), custom_call_target="tpu_custom_call" | custom-call | tf_op jit(solution)/shard_map/cross_and_compress/pallas_call | solution.py:98
  60.5 0.1 collective-permute-start.2
  60.6 0.0 collective-permute-done
  60.6 1.7 %constant_dynamic-slice_fusion.2 = bf16[4,1024,256]{2,1,0:T(8,128)(2,1)S(1)} fusion(bf16[4,1024,512]{2,1,0:T(8,128)(2,1)} %collective-permute-done, s32[]{:T(128)S(6)} %select_n.19), kind=kLoop, calls=%fused_computation.15 | loop fusion | bytes 4194308 | tf_op jit(solution)/shard_map/dynamic_slice | solution.py:180
  62.3 1.0 %fusion.3.early_ref = f32[8,128,256]{2,1,0:T(8,128)S(1)} fusion(bf16[4,1024,256]{2,1,0:T(8,128)(2,1)S(1)} %constant_dynamic-slice_fusion.3, bf16[4,1024,256]{2,1,0:T(8,128)(2,1)S(1)} %constant_dynamic-slice_fusion.2, bf16[128,896]{1,0:T(8,128)(2,1)S(1)} %copy-done), kind=kOutput, calls=%fused_computation.4 | convolution fusion | flops 477102080 | bytes 5472256 | tf_op jit(solution)/shard_map/ri,eih->erh/dot_general | solution.py:183
  63.3 0.0 collective-permute-done.2.other_ref
  63.4 1.3 %mix_experts.1 = bf16[128,1024]{1,0:T(8,128)(2,1)S(1)} custom-call(s32[1]{0:T(128)} %bitcast.tower_ref, f32[8,128,256]{2,1,0:T(8,128)S(1)} %fusion.3.early_ref, bf16[8,128,256]{2,1,0:T(8,128)(2,1)S(1)} %pad_maximum_fusion.late_w_ref, f32[8,256]{1,0:T(8,128)S(1)} %pad_maximum_fusion.1.bias_ref, f32[128,32]{1,0:T(8,128)S(1)} %convolution_bitcast_fusion.gate_early_ref, ...), custom_call_target="tpu_custom_call" | custom-call | tf_op jit(solution)/shard_map/mix_experts/pallas_call | solution.py:138
  64.6 0.9 %reshape.15 = bf16[128,4,256]{2,1,0:T(4,128)(2,1)} reshape(bf16[128,1024]{1,0:T(8,128)(2,1)S(1)} %mix_experts.1) | data formatting | bytes 524288 | tf_op jit(solution)/shard_map/reshape | solution.py:146
  (6 shorter events, 0.1 us)
Async XLA Ops:
  0.0 44.6 %copy-start = (bf16[128,896]{1,0:T(8,128)(2,1)S(1)}, bf16[128,896]{1,0:T(8,128)(2,1)}, u32[]{:S(2)}) copy-start(bf16[128,896]{1,0:T(8,128)(2,1)} %param.20) | copy-start | bytes 688132
  0.0 60.6 %collective-permute-start = (bf16[4,1024,512]{2,1,0:T(8,128)(2,1)}, bf16[4,1024,512]{2,1,0:T(8,128)(2,1)}, u32[]{:S(2)}, u32[]{:S(2)}) collective-permute-start(bf16[4,1024,512]{2,1,0:T(8,128)(2,1)} %param.21), channel_id=1, source_target_pairs={{0,8},{8,0},{1,9},{9,1},{2,10},{10,2},{3,11},{11,3},{4,12},{12,4},... | collective-permute-start | bytes 12582920 | tf_op jit(solution)/shard_map/ppermute | solution.py:168
  0.5 44.6 %collective-permute-start.1 = (f32[4,512]{1,0:T(4,128)}, f32[4,512]{1,0:T(4,128)S(1)}, u32[]{:S(2)}, u32[]{:S(2)}) collective-permute-start(f32[4,512]{1,0:T(4,128)} %param.22), channel_id=1, source_target_pairs={{0,8},{8,0},{1,9},{9,1},{2,10},{10,2},{3,11},{11,3},{4,12},{12,4},... | collective-permute-start | bytes 24584 | tf_op jit(solution)/shard_map/ppermute | solution.py:169
  0.5 2.8 %copy-start.1 = (bf16[1,8,16384,24]{2,3,1,0:T(8,128)(2,1)S(1)}, bf16[1,8,16384,24]{2,3,1,0:T(8,128)(2,1)}, u32[]{:S(2)}) copy-start(bf16[1,8,16384,24]{2,3,1,0:T(8,128)(2,1)} %param.15) | copy-start | bytes 18874372
  3.3 0.9 %copy-start.4 = (s32[1,8,1024,4]{2,3,1,0:T(4,128)S(1)}, s32[1,8,1024,4]{2,3,1,0:T(4,128)}, u32[]{:S(2)}) copy-start(s32[1,8,1024,4]{2,3,1,0:T(4,128)} %param.12) | copy-start | bytes 393220
  4.2 0.8 %copy-start.5 = (s32[1,8,1024]{2,1,0:T(8,128)S(1)}, s32[1,8,1024]{2,1,0:T(8,128)}, u32[]{:S(2)}) copy-start(s32[1,8,1024]{2,1,0:T(8,128)} %param.13) | copy-start | bytes 98308
  5.0 37.8 %copy-start.9 = (bf16[1024,4,8]{0,2,1:T(8,128)(2,1)S(1)}, bf16[1024,4,8]{0,2,1:T(8,128)(2,1)}, u32[]{:S(2)}) copy-start(bf16[1024,4,8]{0,2,1:T(8,128)(2,1)} %param.23) | copy-start | bytes 196612
  35.3 9.5 %copy-start.10 = (f32[4,512]{1,0:T(4,128)S(1)}, f32[4,512]{1,0:T(4,128)}, u32[]{:S(2)}) copy-start(f32[4,512]{1,0:T(4,128)} %param.22) | copy-start | bytes 24580
  35.3 19.3 %copy-start.3 = (bf16[1,1536,64]{1,2,0:T(8,128)(2,1)S(1)}, bf16[1,1536,64]{1,2,0:T(8,128)(2,1)}, u32[]{:S(2)}) copy-start(bf16[1,1536,64]{1,2,0:T(8,128)(2,1)} %param.18) | copy-start | bytes 589828
  35.3 19.3 %copy-start.6 = (f32[1,1536]{1,0:T(1,128)S(1)}, f32[1,1536]{1,0:T(1,128)}, u32[]{:S(2)}) copy-start(f32[1,1536]{1,0:T(1,128)} %bias_ref.1) | copy-start | bytes 18436
  35.3 19.3 %copy-start.7 = (s32[1,64]{1,0:T(1,128)S(1)}, s32[1,64]{1,0:T(1,128)}, u32[]{:S(2)}) copy-start(s32[1,64]{1,0:T(1,128)} %param.14) | copy-start | bytes 772
  35.3 19.3 %copy-start.8 = (f32[1,64]{1,0:T(1,128)S(1)}, f32[1,64]{1,0:T(1,128)}, u32[]{:S(2)}) copy-start(f32[1,64]{1,0:T(1,128)} %comp_bias_ref.1) | copy-start | bytes 772
  35.3 19.3 %all-to-all-start = ((bf16[8,8,24,128]{3,2,1,0:T(8,128)(2,1)}), bf16[8,8,24,128]{3,2,1,0:T(8,128)(2,1)S(1)}, u32[]{:S(2)}, u32[]{:S(2)}) async-start(bf16[8,8,24,128]{3,2,1,0:T(8,128)(2,1)} %pool_features.1), calls=%async_computation | async-start | bytes 786432 | tf_op jit(solution)/shard_map/all_to_all | solution.py:174
  54.7 2.3 %copy-start.2 = (bf16[1,1536,1536]{2,1,0:T(8,128)(2,1)S(1)}, bf16[1,1536,1536]{2,1,0:T(8,128)(2,1)}, u32[]{:S(2)}) copy-start(bf16[1,1536,1536]{2,1,0:T(8,128)(2,1)} %param.16) | copy-start | bytes 14155780
  60.5 2.8 %collective-permute-start.2 = (bf16[128,64]{1,0:T(8,128)(2,1)S(1)}, bf16[128,64]{1,0:T(8,128)(2,1)S(1)}, u32[]{:S(2)}, u32[]{:S(2)}) collective-permute-start(bf16[128,64]{1,0:T(8,128)(2,1)S(1)} %cross_and_compress.1.own_ref), channel_id=1, source_target_pairs={{0,8},{8,0},{1,9},{9,1},{2,10},{10,2},{3,11},{11,3},{4,12},{12,4},... | collective-permute-start | bytes 49160 | tf_op jit(solution)/shard_map/ppermute | solution.py:193

commit v2 on v1

v2 whole, which is shorter than its diff:
```python
import functools

import jax
import jax.numpy as jnp
from jax import lax
from jax.experimental import pallas as pl
from jax.experimental.pallas import tpu as pltpu
from jax.sharding import PartitionSpec as P

LOW = 256
CHUNKS = 4


def pool_kernel(by_row, tile, row_count, groups, *refs):
    ids_hbm, len_hbm, tab_hbm, out_ref, ids_ref, len_ref, tab, table_low, sem = refs[:9]
    features, embed, vocab = tab.shape
    bag, samples = ids_ref.shape[1], ids_ref.shape[2]
    high = vocab // LOW
    copies = [pltpu.make_async_copy(ids_hbm, ids_ref, sem.at[0]), pltpu.make_async_copy(len_hbm, len_ref, sem.at[1])]
    for copy in copies:
        copy.start()
    parts = []
    if by_row:
        row_ref, pooled, shown, sem_ids = refs[9:13]
        addresses = refs[13:]
        width = vocab // CHUNKS
        for c in range(CHUNKS):
            where = (pl.ds(0, by_row), slice(None), pl.ds(c * width, width))
            parts.append(pltpu.make_async_copy(tab_hbm.at[where], tab.at[where], sem.at[3 + c]))
            parts[-1].start()
    others = pl.ds(by_row, features - by_row)
    rest_copy = pltpu.make_async_copy(tab_hbm.at[others], tab.at[others], sem.at[2])
    rest_copy.start()
    for copy in copies:
        copy.wait()
    if by_row:
        for f in range(by_row):
            for j in range(bag):
                shown[f * bag + j] = jnp.where(j < len_ref[pl.ds(f, 1), :], ids_ref[f, pl.ds(j, 1), :], vocab)
        moves = [pltpu.make_async_copy(shown.at[n, 0], addresses[n], sem_ids.at[n]) for n in range(by_row * bag)]
        for move in moves:
            move.start()
        row_ref[pl.ds(vocab, 8), :] = jnp.zeros((8, 128), jnp.float32)
        square = [lax.broadcasted_iota(jnp.int32, (LOW, LOW), axis) for axis in range(2)]
        unit = (square[0] == square[1]).astype(jnp.float32).astype(jnp.bfloat16)
        blank = jnp.zeros((128 - by_row * embed, LOW), jnp.float32)

        def build(block, carry, first):
            start = pl.multiple_of(first + block * 2 * LOW, 2 * LOW)
            both = []
            for n in range(2):
                both += [tab[f, :, pl.ds(start + n * LOW, LOW)].astype(jnp.float32) for f in range(by_row)] + [blank]
            columns = jnp.concatenate(both, axis=0).astype(jnp.bfloat16)
            turned = lax.dot_general(unit, columns, (((1,), (1,)), ((), ())), preferred_element_type=jnp.float32)
            row_ref[pl.ds(start, LOW), :] = turned[:, :128]
            row_ref[pl.ds(start + LOW, LOW), :] = turned[:, 128:]
            return carry

        for c in range(CHUNKS):
            parts[c].wait()
            lax.fori_loop(0, width // (2 * LOW), functools.partial(build, first=c * width), 0, unroll=4)
        for move in moves:
            move.wait()
    rest_copy.wait()
    lane = lax.broadcasted_iota(jnp.int32, (1, 128), 1)

    def lookups(group):
        row = pl.multiple_of(group * 8, 8)
        for u in range(8):
            line = None
            for f in range(by_row):
                found = [row_ref[pl.ds(addresses[f * bag + j][row + u], 1), :] for j in range(bag)]
                total = found[0]
                for item in found[1:]:
                    total = total + item
                line = total if line is None else jnp.where(lane < embed * f, line, total)
                yield
            pooled[pl.ds(row + u, 1), :] = line

    level = lax.broadcasted_iota(jnp.int32, (LOW, tile), 0)
    tiles = samples // tile
    last = samples // 8 - 1

    def step(i, carry):
        feature, t = by_row + i // tiles, i % tiles
        start = pl.multiple_of(t * tile, tile)

        def arrange():
            for part in range(0, high, 2):
                pair = [tab[feature, :, pl.ds((part + n) * LOW, LOW)].astype(jnp.float32) for n in range(2)]
                table_low[pl.ds(part * embed, 2 * embed), :] = jnp.concatenate(pair, axis=0).astype(jnp.bfloat16)

        pl.when(t == 0)(arrange)
        work = (item for g in range(groups) for item in lookups(jnp.minimum(i * groups + g, last)))
        wanted = groups * 8 * by_row
        given, selects = 0, 0
        length = len_ref[pl.ds(feature, 1), pl.ds(start, tile)]
        total = jnp.zeros((embed, tile), jnp.float32)
        for slot in range(bag):
            index = ids_ref[feature, pl.ds(slot, 1), pl.ds(start, tile)]
            upper = jnp.where(slot < length, index // LOW, -1)
            chosen = (level == index % LOW).astype(jnp.float32).astype(jnp.bfloat16)
            found = jnp.dot(table_low[...], chosen, preferred_element_type=jnp.float32)
            picked = jnp.zeros((embed, tile), jnp.float32)
            for part in range(high):
                picked = jnp.where(upper == part, found[part * embed : (part + 1) * embed], picked)
                selects += 1
                while given * bag * high < selects * wanted:
                    next(work, None)
                    given += 1
            total = total + picked
        for _ in work:
            pass
        for block in range(tile // row_count):
            piece = total[:, block * row_count : (block + 1) * row_count]
            out_ref[t * (tile // row_count) + block, feature] = piece.astype(jnp.bfloat16)
        return carry

    steps = (features - by_row) * tiles
    lax.fori_loop(0, steps, step, 0)
    if by_row:

        def rest(group, carry):
            for _ in lookups(group):
                pass
            return carry

        lax.fori_loop(min(steps * groups, last + 1), last + 1, rest, 0)
        for block in range(samples // row_count):
            turned = pooled[pl.ds(block * row_count, row_count), :].T
            for f in range(by_row):
                out_ref[block, f] = turned[f * embed : (f + 1) * embed].astype(jnp.bfloat16)


def pool_features(table, ids, lengths, inner_size):
    features, embed, vocab = table.shape
    bag, samples = ids.shape[1], ids.shape[2]
    row_count = samples // inner_size
    tile = row_count * max(1, min(samples, 1024) // row_count)
    by_row = min(128 // embed, features * 5 // 8)
    steps = (features - by_row) * (samples // tile)
    groups = samples // 8 // steps * 15 // 16 if by_row else 0
    hbm = pl.BlockSpec(memory_space=pltpu.HBM)
    scratch = [
        pltpu.VMEM(ids.shape, jnp.int32),
        pltpu.VMEM(lengths.shape, jnp.int32),
        pltpu.VMEM(table.shape, jnp.bfloat16),
        pltpu.VMEM((vocab // LOW * embed, LOW), jnp.bfloat16),
        pltpu.SemaphoreType.DMA((3 + CHUNKS,)),
    ]
    if by_row:
        scratch += [
            pltpu.VMEM((vocab + 8, 128), jnp.float32),
            pltpu.VMEM((samples, 128), jnp.float32),
            pltpu.VMEM((by_row * bag, 1, samples), jnp.int32),
            pltpu.SemaphoreType.DMA((by_row * bag,)),
        ] + [pltpu.SMEM((samples,), jnp.int32)] * (by_row * bag)
    return pl.pallas_call(
        functools.partial(pool_kernel, by_row, tile, row_count, groups),
        out_shape=jax.ShapeDtypeStruct((inner_size, features, embed, row_count), jnp.bfloat16),
        in_specs=[hbm, hbm, hbm],
        out_specs=pl.BlockSpec(memory_space=pltpu.VMEM),
        scratch_shapes=scratch,
        compiler_params=pltpu.CompilerParams(vmem_limit_bytes=48 * 2**20),
        name="pool_features",
    )(ids, lengths, table)


def early_kernel(known, tower_ref, other_ref, own_hbm, far_hbm, own_bias_ref, far_bias_ref, gate_ref, cross_hbm, *refs):
    early_ref, gate_early_ref, late_ref, gate_late_ref, cross_ref, weights, sem = refs
    tower = tower_ref[0]
    half, experts_in, columns = own_hbm.shape[0], weights.shape[1], weights.shape[2]
    span = pl.ds(pl.multiple_of(tower * columns, columns), columns)
    copies = []
    for n, (source, place) in enumerate([(own_hbm, tower), (far_hbm, 1 - tower)]):
        for e in range(half):
            copies.append(
                pltpu.make_async_copy(source.at[e, :, span], weights.at[place * half + e], sem.at[n * half + e])
            )
            copies[-1].start()
    cross_copy = pltpu.make_async_copy(cross_hbm, cross_ref, sem.at[2 * half])
    cross_copy.start()
    tasks, experts, depth = gate_ref.shape
    gates = gate_ref[...].astype(jnp.float32).reshape(tasks * experts, depth).astype(jnp.bfloat16)
    gate_early_ref[...] = lax.dot_general(
        other_ref[...], gates[:, :known], (((1,), (1,)), ((), ())), preferred_element_type=jnp.float32
    )
    gate_late_ref[...] = gates[:, known:]
    for n, (bias, place) in enumerate([(own_bias_ref, tower), (far_bias_ref, 1 - tower)]):
        for e in range(half):
            copies[n * half + e].wait()
            at = place * half + e
            found = jnp.dot(other_ref[...], weights[at, pl.ds(0, known), :], preferred_element_type=jnp.float32)
            early_ref[at] = found + bias[pl.ds(e, 1), span]
            late_ref[at] = weights[at, pl.ds(known, experts_in - known), :]
    cross_copy.wait()


def early_part(tower, other, own_w, far_w, own_b, far_b, gates, cross_w):
    half, depth, hidden = own_w.shape
    rows, known = other.shape
    columns = hidden // 2
    vmem, hbm = pl.BlockSpec(memory_space=pltpu.VMEM), pl.BlockSpec(memory_space=pltpu.HBM)
    count = gates.shape[0] * gates.shape[1]
    return pl.pallas_call(
        functools.partial(early_kernel, known),
        out_shape=(
            jax.ShapeDtypeStruct((2 * half, rows, columns), jnp.float32),
            jax.ShapeDtypeStruct((rows, count), jnp.float32),
            jax.ShapeDtypeStruct((2 * half, depth - known, columns), jnp.bfloat16),
            jax.ShapeDtypeStruct((count, depth - known), jnp.bfloat16),
            jax.ShapeDtypeStruct(cross_w.shape, jnp.bfloat16),
        ),
        in_specs=[pl.BlockSpec(memory_space=pltpu.SMEM), vmem, hbm, hbm, vmem, vmem, vmem, hbm],
        out_specs=(vmem,) * 5,
        scratch_shapes=[pltpu.VMEM((2 * half, depth, columns), jnp.bfloat16), pltpu.SemaphoreType.DMA((2 * half + 1,))],
        compiler_params=pltpu.CompilerParams(vmem_limit_bytes=24 * 2**20),
        cost_estimate=pl.CostEstimate(
            flops=4 * half * rows * known * columns,
            bytes_accessed=2 * (2 * half * depth * columns + cross_w.size),
            transcendentals=0,
        ),
        name="early_part",
    )(tower, other, own_w, far_w, own_b, far_b, gates, cross_w)


def cross_kernel(blocks, slot_ref, rec_ref, w_ref, bias_ref, comp_ref, comp_bias_ref, out_ref, first_t, first):
    slots, embed, rows = rec_ref.shape
    width = w_ref.shape[1]
    step = width // blocks
    for f in range(slots):
        first_t[slot_ref[f]] = rec_ref[f].astype(jnp.float32)
    first[...] = first_t[...].reshape(width, rows).T.astype(jnp.bfloat16)
    total = jnp.zeros((rows, comp_ref.shape[0]), jnp.float32) + comp_bias_ref[...]
    for n in range(blocks):
        span = pl.ds(n * step, step)
        crossed = jnp.dot(first[...], w_ref[:, span], preferred_element_type=jnp.float32) + bias_ref[:, span]
        base = first[:, span].astype(jnp.float32)
        second = (base * crossed + base).astype(jnp.bfloat16)
        total = total + lax.dot_general(
            second, comp_ref[:, span], (((1,), (1,)), ((), ())), preferred_element_type=jnp.float32
        )
    out_ref[...] = total.astype(jnp.bfloat16)


def cross_and_compress(received, slots, cross_w, cross_b, comp_w, comp_b):
    slot_total, embed, rows = received.shape
    width = cross_w.shape[0]
    vmem = pl.BlockSpec(memory_space=pltpu.VMEM)
    return pl.pallas_call(
        functools.partial(cross_kernel, width // 256),
        out_shape=jax.ShapeDtypeStruct((rows, comp_w.shape[1]), jnp.bfloat16),
        in_specs=[pl.BlockSpec(memory_space=pltpu.SMEM), vmem, vmem, vmem, vmem, vmem],
        out_specs=vmem,
        scratch_shapes=[
            pltpu.VMEM((slot_total, embed, rows), jnp.float32),
            pltpu.VMEM((rows, width), jnp.bfloat16),
        ],
        compiler_params=pltpu.CompilerParams(vmem_limit_bytes=16 * 2**20),
        name="cross_and_compress",
    )(slots, received, cross_w, cross_b, comp_w.T, comp_b)


def mix_kernel(tower_ref, early_ref, late_ref, gate_early_ref, gate_late_ref, own_ref, far_ref, out_ref):
    experts, rows, columns = early_ref.shape
    tasks = gate_early_ref.shape[1] // experts
    own, far = own_ref[...], far_ref[...]
    lead = tower_ref[0] == 0
    squeezed = jnp.concatenate([jnp.where(lead, own, far), jnp.where(lead, far, own)], axis=1)
    logits = gate_early_ref[...] + lax.dot_general(
        squeezed, gate_late_ref[...], (((1,), (1,)), ((), ())), preferred_element_type=jnp.float32
    )
    weights = jnp.exp(logits)
    probs = []
    for k in range(tasks):
        mine = weights[:, k * experts : (k + 1) * experts]
        probs.append(mine / jnp.sum(mine, axis=1, keepdims=True))
    totals = [jnp.zeros((rows, columns), jnp.float32) for _ in range(tasks)]
    for e in range(experts):
        hidden = early_ref[e] + jnp.dot(squeezed, late_ref[e], preferred_element_type=jnp.float32)
        hidden = jnp.maximum(hidden, 0.0).astype(jnp.bfloat16).astype(jnp.float32)
        for k in range(tasks):
            totals[k] = totals[k] + probs[k][:, e : e + 1] * hidden
    out_ref[...] = jnp.stack(totals, axis=1).astype(jnp.bfloat16)


def mix_experts(tower, early, late, gate_early, gate_late, own, far):
    experts, rows, columns = early.shape
    tasks = gate_early.shape[1] // experts
    vmem = pl.BlockSpec(memory_space=pltpu.VMEM)
    return pl.pallas_call(
        mix_kernel,
        out_shape=jax.ShapeDtypeStruct((rows, tasks, columns), jnp.bfloat16),
        in_specs=[pl.BlockSpec(memory_space=pltpu.SMEM)] + [vmem] * 6,
        out_specs=vmem,
        compiler_params=pltpu.CompilerParams(vmem_limit_bytes=16 * 2**20),
        name="mix_experts",
    )(tower, early, late, gate_early, gate_late, own, far)


def on_device(
    ids,
    bag_len,
    slot_of_feature,
    tables,
    cross_w,
    cross_b,
    comp_w,
    comp_b,
    other_towers,
    expert_w,
    expert_b,
    gate_w,
):
    inner_size = lax.axis_size("inner")
    tower_size = lax.axis_size("tower")
    tower = lax.axis_index("tower")
    swap = [(n, (n + 1) % tower_size) for n in range(tower_size)]

    far_w = lax.ppermute(expert_w, "tower", swap)
    far_b = lax.ppermute(expert_b, "tower", swap)

    pooled = pool_features(
        jnp.transpose(tables[0], (0, 2, 1)), jnp.transpose(ids[0], (0, 2, 1)), bag_len[0], inner_size
    )
    received = lax.all_to_all(pooled, "inner", split_axis=0, concat_axis=0, tiled=True)
    received = received.reshape((-1,) + received.shape[2:])

    place = tower.reshape(1)
    gates = jnp.transpose(gate_w, (1, 2, 0))
    early = early_part(place, other_towers, expert_w, far_w, expert_b, far_b, gates, cross_w[0])
    received, early = lax.optimization_barrier((received, early))
    hidden_early, gate_early, late_w, gate_late, near_w = early

    squeezed = cross_and_compress(received, slot_of_feature[0], near_w, cross_b, comp_w[0], comp_b)
    opposite = lax.ppermute(squeezed, "tower", swap)
    return mix_experts(place, hidden_early, late_w, gate_early, gate_late, squeezed, opposite)


def solution(mesh):
    return jax.shard_map(
        on_device,
        mesh=mesh,
        in_specs=(
            P("tower", "inner", "groups", None),
            P("tower", "inner", "groups"),
            P("tower", None),
            P("tower", "inner", None, None),
            P("tower", None, None),
            P("tower", None),
            P("tower", None, None),
            P("tower", None),
            P(("groups", "inner"), None),
            P("tower", None, None),
            P("tower", None),
            P(),
        ),
        out_specs=P(("groups", "inner"), None, "tower"),
        check_vma=False,
    )
```

time: 66 us -> 49.1 us (0.74)
  Pallas kernels: 35.1 us -> 26.8 us
  waiting for transfers between devices: 9.6 us -> 3.49 us
  matrix products: 1.15 us -> 0 us
  local copies, waits for them, and re-layouts: 11.4 us -> 10.7 us
    all_to_all x1, waiting for transfers between devices: 9.59 us -> 1.2 us  [on_device(): lax.all_to_all(pooled, 'inner', split_axis=0, concat_axis=0, tiled=True)]
    pallas_call x3 -> x4, Pallas kernels: 35.1 us -> 26.8 us  [the longest x1 19.4 us: pool_features(): pl.pallas_call(functools.partial(pool_kernel, by_row, tile, row_count, gr...]
    unnamed x23 -> x26, local copies, waits for them, and re-layouts: 6.93 us -> 10.7 us
    dynamic_slice x5 -> x0, local copies, waits for them, and re-layouts: 3.54 us -> none  [the longest x4 3.49 us: on_device(): lax.dynamic_slice_in_dim(x, tower * columns, columns, axis=x.ndim - 1)]
    ppermute x1, waiting for transfers between devices: 0.01 us -> 1.19 us  [on_device(): opposite = lax.ppermute(squeezed, 'tower', swap)]
    dot_general x2 -> x0, matrix products: 1.15 us -> none  [the longest x1 0.95 us: on_device(): jnp.einsum('ri,eih->erh', other_towers, both_w[:, :known], preferred_elem...]
    ppermute x1, waiting for transfers between devices: 0.01 us -> 1.09 us  [on_device(): far_b = lax.ppermute(expert_b, 'tower', swap)]
    reshape x2 -> x0, local copies, waits for them, and re-layouts: 0.9 us -> none  [the longest x1 0.88 us: mix_experts(): return out.reshape(rows, tasks, columns)]
  transfers between devices with their start and end apart: 4 -> 4, of which waited for: 1 -> 3; matrix products, arithmetic and copies ran while one was open for 8% -> 0% of each run, Pallas kernels for 52% -> 46%
where the time goes in v2:
time: 49.1 us; the launch traced here: 48.6 us
  Pallas kernels  26.8 us (55%)
  local copies, waits for them, and re-layouts  10.7 us (22%)
  starting transfers between devices  7.64 us (16%)
  waiting for transfers between devices  3.49 us (7%)
    pallas_call x1, Pallas kernels, pool_features(): pl.pallas_call(functools.partial(pool_kernel, by_row, tile, row_count, gr...  19.4 us
    unnamed x26, local copies, waits for them, and re-layouts  10.7 us
    all_to_all x1, starting transfers between devices, on_device(): lax.all_to_all(pooled, 'inner', split_axis=0, concat_axis=0, tiled=True)  6.97 us
    pallas_call x1, Pallas kernels, early_part(): pl.pallas_call(functools.partial(early_kernel, known), out_shape=(jax.Sha...  3.07 us
    pallas_call x1, Pallas kernels, mix_experts(): pl.pallas_call(mix_kernel, out_shape=jax.ShapeDtypeStruct((rows, tasks, c...  2.2 us
    pallas_call x1, Pallas kernels, cross_and_compress(): pl.pallas_call(functools.partial(cross_kernel, width // 256), out_shape=j...  2.12 us
    all_to_all x1, waiting for transfers between devices, on_device(): lax.all_to_all(pooled, 'inner', split_axis=0, concat_axis=0, tiled=True)  1.2 us
    ppermute x1, waiting for transfers between devices, on_device(): opposite = lax.ppermute(squeezed, 'tower', swap)  1.19 us
  transfers between devices with their start and end apart: 4, of which 3 were waited for; matrix products, arithmetic and copies ran while one was open for 0% of the time, Pallas kernels for 46%

profile of v2, /device:TPU:0, one launch (start us, length us, event | category | flops | bytes accessed | tf_op | source)
XLA Modules:
  0.0 48.6 jit_solution(2108387399096759369)
XLA Ops:
  0.0 0.0 copy-start.4
  0.0 0.5 collective-permute-start
  0.5 0.0 copy-start.6
  0.5 0.9 %copy-done.6 = s32[1,8,1024,4]{2,3,1,0:T(4,128)S(1)} copy-done((s32[1,8,1024,4]{2,3,1,0:T(4,128)S(1)}, s32[1,8,1024,4]{2,3,1,0:T(4,128)}, u32[]{:S(2)}) %copy-start.6) | copy-done | bytes 131096
  1.4 0.0 copy-start.8
  1.4 0.8 %copy-done.8 = s32[1,8,1024]{2,1,0:T(8,128)S(1)} copy-done((s32[1,8,1024]{2,1,0:T(8,128)S(1)}, s32[1,8,1024]{2,1,0:T(8,128)}, u32[]{:S(2)}) %copy-start.8) | copy-done | bytes 32792
  2.1 0.0 copy-start.9
  2.1 0.0 copy-start.7
  2.1 19.4 %pool_features.1 = bf16[8,8,24,128]{3,2,1,0:T(8,128)(2,1)} custom-call(s32[8,4,1024]{2,1,0:T(4,128)S(1)} %bitcast.18, s32[8,1024]{1,0:T(8,128)S(1)} %bitcast.20, bf16[8,24,16384]{2,1,0:T(8,128)(2,1)} %bitcast.22), custom_call_target="tpu_custom_call" | custom-call | tf_op jit(solution)/shard_map/pool_features/pallas_call | solution.py:158
  21.5 7.0 %all-to-all-start = ((bf16[8,8,24,128]{3,2,1,0:T(8,128)(2,1)}), bf16[8,8,24,128]{3,2,1,0:T(8,128)(2,1)S(1)}, u32[]{:S(2)}, u32[]{:S(2)}) async-start(bf16[8,8,24,128]{3,2,1,0:T(8,128)(2,1)} %pool_features.1), calls=%async_computation | async-start | bytes 786432 | tf_op jit(solution)/shard_map/all_to_all | solution.py:326
  28.5 0.0 copy-done.9
  28.5 0.1 collective-permute-start.1
  28.6 1.1 %collective-permute-done.1.far_bias_ref = f32[4,512]{1,0:T(4,128)S(1)} collective-permute-done((f32[4,512]{1,0:T(4,128)S(1)}, f32[4,512]{1,0:T(4,128)S(1)}, u32[]{:S(2)}, u32[]{:S(2)}) %collective-permute-start.1) | collective-permute-done | bytes 8224 | tf_op jit(solution)/shard_map/ppermute | solution.py:321
  29.7 0.0 collective-permute-done.far_hbm
  29.7 0.0 copy-done.4
  29.7 0.0 copy-done.7
  29.7 0.0 copy-start
  29.7 2.3 %copy-done = bf16[1,1536,1536]{2,1,0:T(8,128)(2,1)S(1)} copy-done((bf16[1,1536,1536]{2,1,0:T(8,128)(2,1)S(1)}, bf16[1,1536,1536]{2,1,0:T(8,128)(2,1)}, u32[]{:S(2)}) %copy-start) | copy-done | bytes 4718616
  32.1 0.0 copy-start.3
  32.1 2.2 %copy-done.3 = bf16[4,1024,512]{2,1,0:T(8,128)(2,1)S(1)} copy-done((bf16[4,1024,512]{2,1,0:T(8,128)(2,1)S(1)}, bf16[4,1024,512]{2,1,0:T(8,128)(2,1)}, u32[]{:S(2)}) %copy-start.3) | copy-done | bytes 4194328
  34.3 0.0 copy-start.5
  34.3 0.0 copy-start.10
  34.3 0.0 copy-start.11
  34.3 0.0 copy-start.12
  34.3 3.1 %early_part.1 = (f32[8,128,256]{2,1,0:T(8,128)S(1)}, f32[128,32]{1,0:T(8,128)S(1)}, bf16[8,128,256]{2,1,0:T(8,128)(2,1)S(1)}, bf16[32,128]{1,0:T(8,128)(2,1)S(1)}, bf16[1536,1536]{1,0:T(8,128)(2,1)S(1)}) custom-call(s32[1]{0:T(128)} %bitcast.tower_ref, bf16[128,896]{1,0:T(8,128)(2,1)S(1)} %copy-done.4, bf16[4,1024,512]{2,1,0:T(8,128)(2,1)S(1)} %copy-done.3, ...), custom_call_target="tpu_custom_call" | custom-call | flops 469762048 | bytes 8912896 | tf_op jit(solution)/shard_map/early_part/pallas_call | solution.py:205
  37.4 0.0 copy-start.1
  37.4 2.1 %copy-done.1 = bf16[1536,1536]{1,0:T(8,128)(2,1)} copy-done((bf16[1536,1536]{1,0:T(8,128)(2,1)}, bf16[1536,1536]{1,0:T(8,128)(2,1)S(1)}, u32[]{:S(2)}) %copy-start.1) | copy-done | bytes 4718616
  39.5 1.2 %all-to-all-done = bf16[8,8,24,128]{3,2,1,0:T(8,128)(2,1)S(1)} async-done(((bf16[8,8,24,128]{3,2,1,0:T(8,128)(2,1)}), bf16[8,8,24,128]{3,2,1,0:T(8,128)(2,1)S(1)}, u32[]{:S(2)}, u32[]{:S(2)}) %all-to-all-start) | async-done | bytes 393248 | tf_op jit(solution)/shard_map/all_to_all | solution.py:326
  40.7 0.0 copy-done.5
  40.7 0.0 copy-done.10
  40.7 0.0 copy-done.11
  40.7 0.0 copy-done.12
  40.7 0.0 copy-start.2
  40.7 2.3 %copy-done.2 = bf16[1536,1536]{1,0:T(8,128)(2,1)S(1)} copy-done((bf16[1536,1536]{1,0:T(8,128)(2,1)S(1)}, bf16[1536,1536]{1,0:T(8,128)(2,1)}, u32[]{:S(2)}) %copy-start.2) | copy-done | bytes 4718616
  43.0 2.1 %cross_and_compress.1.own_ref = bf16[128,64]{1,0:T(8,128)(2,1)S(1)} custom-call(s32[64]{0:T(128)S(1)} %bitcast.21, bf16[64,24,128]{2,1,0:T(8,128)(2,1)S(1)} %bitcast.16, bf16[1536,1536]{1,0:T(8,128)(2,1)S(1)} %copy-done.2, f32[1,1536]{1,0:T(1,128)S(1)} %copy-done.10, bf16[64,1536]{1,0:T(8,128)(2,1)S(1)} %bitcast.17, f32[1,64]{1,0:T(1,128)S(1)} %copy-done.12), custom_call_target="tpu_custom_call" | custom-call | tf_op jit(solution)/shard_map/cross_and_compress/pallas_call | solution.py:250
  45.2 0.1 collective-permute-start.2
  45.2 1.2 %collective-permute-done.2.far_ref = bf16[128,64]{1,0:T(8,128)(2,1)S(1)} collective-permute-done((bf16[128,64]{1,0:T(8,128)(2,1)S(1)}, bf16[128,64]{1,0:T(8,128)(2,1)S(1)}, u32[]{:S(2)}, u32[]{:S(2)}) %collective-permute-start.2) | collective-permute-done | bytes 16416 | tf_op jit(solution)/shard_map/ppermute | solution.py:336
  46.4 2.2 %mix_experts.1 = bf16[128,4,256]{2,1,0:T(4,128)(2,1)} custom-call(s32[1]{0:T(128)} %bitcast.tower_ref, f32[8,128,256]{2,1,0:T(8,128)S(1)} %get-tuple-element.21.early_ref, bf16[8,128,256]{2,1,0:T(8,128)(2,1)S(1)} %get-tuple-element.22.late_ref, f32[128,32]{1,0:T(8,128)S(1)} %get-tuple-element.23.gate_early_ref, ...), custom_call_target="tpu_custom_call" | custom-call | tf_op jit(solution)/shard_map/mix_experts/pallas_call | solution.py:291
Async XLA Ops:
  0.0 29.7 %copy-start.4 = (bf16[128,896]{1,0:T(8,128)(2,1)S(1)}, bf16[128,896]{1,0:T(8,128)(2,1)}, u32[]{:S(2)}) copy-start(bf16[128,896]{1,0:T(8,128)(2,1)} %other_ref.1) | copy-start | bytes 688132
  0.0 29.7 %collective-permute-start = (bf16[4,1024,512]{2,1,0:T(8,128)(2,1)}, bf16[4,1024,512]{2,1,0:T(8,128)(2,1)}, u32[]{:S(2)}, u32[]{:S(2)}) collective-permute-start(bf16[4,1024,512]{2,1,0:T(8,128)(2,1)} %own_hbm.1), channel_id=1, source_target_pairs={{0,8},{8,0},{1,9},{9,1},{2,10},{10,2},{3,11},{11,3},{4,12},{12,4},... | collective-permute-start | bytes 12582920 | tf_op jit(solution)/shard_map/ppermute | solution.py:320
  0.5 0.9 %copy-start.6 = (s32[1,8,1024,4]{2,3,1,0:T(4,128)S(1)}, s32[1,8,1024,4]{2,3,1,0:T(4,128)}, u32[]{:S(2)}) copy-start(s32[1,8,1024,4]{2,3,1,0:T(4,128)} %param.12) | copy-start | bytes 393220
  1.4 0.8 %copy-start.8 = (s32[1,8,1024]{2,1,0:T(8,128)S(1)}, s32[1,8,1024]{2,1,0:T(8,128)}, u32[]{:S(2)}) copy-start(s32[1,8,1024]{2,1,0:T(8,128)} %param.13) | copy-start | bytes 98308
  2.1 26.4 %copy-start.9 = (f32[4,512]{1,0:T(4,128)S(1)}, f32[4,512]{1,0:T(4,128)}, u32[]{:S(2)}) copy-start(f32[4,512]{1,0:T(4,128)} %own_bias_ref.1) | copy-start | bytes 24580
  2.1 27.6 %copy-start.7 = (bf16[1024,4,8]{0,2,1:T(8,128)(2,1)S(1)}, bf16[1024,4,8]{0,2,1:T(8,128)(2,1)}, u32[]{:S(2)}) copy-start(bf16[1024,4,8]{0,2,1:T(8,128)(2,1)} %param.23) | copy-start | bytes 196612
  21.5 19.2 %all-to-all-start = ((bf16[8,8,24,128]{3,2,1,0:T(8,128)(2,1)}), bf16[8,8,24,128]{3,2,1,0:T(8,128)(2,1)S(1)}, u32[]{:S(2)}, u32[]{:S(2)}) async-start(bf16[8,8,24,128]{3,2,1,0:T(8,128)(2,1)} %pool_features.1), calls=%async_computation | async-start | bytes 786432 | tf_op jit(solution)/shard_map/all_to_all | solution.py:326
  28.5 1.2 %collective-permute-start.1 = (f32[4,512]{1,0:T(4,128)S(1)}, f32[4,512]{1,0:T(4,128)S(1)}, u32[]{:S(2)}, u32[]{:S(2)}) collective-permute-start(f32[4,512]{1,0:T(4,128)S(1)} %copy-done.9), channel_id=1, source_target_pairs={{0,8},{8,0},{1,9},{9,1},{2,10},{10,2},{3,11},{11,3},{4,12},{12,4},... | collective-permute-start | bytes 24584 | tf_op jit(solution)/shard_map/ppermute | solution.py:321
  29.7 2.3 %copy-start = (bf16[1,1536,1536]{2,1,0:T(8,128)(2,1)S(1)}, bf16[1,1536,1536]{2,1,0:T(8,128)(2,1)}, u32[]{:S(2)}) copy-start(bf16[1,1536,1536]{2,1,0:T(8,128)(2,1)} %param.16) | copy-start | bytes 14155780
  32.1 2.2 %copy-start.3 = (bf16[4,1024,512]{2,1,0:T(8,128)(2,1)S(1)}, bf16[4,1024,512]{2,1,0:T(8,128)(2,1)}, u32[]{:S(2)}) copy-start(bf16[4,1024,512]{2,1,0:T(8,128)(2,1)} %own_hbm.1) | copy-start | bytes 12582916
  34.3 6.4 %copy-start.5 = (bf16[1,1536,64]{1,2,0:T(8,128)(2,1)S(1)}, bf16[1,1536,64]{1,2,0:T(8,128)(2,1)}, u32[]{:S(2)}) copy-start(bf16[1,1536,64]{1,2,0:T(8,128)(2,1)} %param.18) | copy-start | bytes 589828
  34.3 6.4 %copy-start.10 = (f32[1,1536]{1,0:T(1,128)S(1)}, f32[1,1536]{1,0:T(1,128)}, u32[]{:S(2)}) copy-start(f32[1,1536]{1,0:T(1,128)} %bias_ref.1) | copy-start | bytes 18436
  34.3 6.4 %copy-start.11 = (s32[1,64]{1,0:T(1,128)S(1)}, s32[1,64]{1,0:T(1,128)}, u32[]{:S(2)}) copy-start(s32[1,64]{1,0:T(1,128)} %param.14) | copy-start | bytes 772
  34.3 6.4 %copy-start.12 = (f32[1,64]{1,0:T(1,128)S(1)}, f32[1,64]{1,0:T(1,128)}, u32[]{:S(2)}) copy-start(f32[1,64]{1,0:T(1,128)} %comp_bias_ref.1) | copy-start | bytes 772
  37.4 2.1 %copy-start.1 = (bf16[1536,1536]{1,0:T(8,128)(2,1)}, bf16[1536,1536]{1,0:T(8,128)(2,1)S(1)}, u32[]{:S(2)}) copy-start(bf16[1536,1536]{1,0:T(8,128)(2,1)S(1)} %get-tuple-element.26.w_ref) | copy-start | bytes 14155780
  40.7 2.3 %copy-start.2 = (bf16[1536,1536]{1,0:T(8,128)(2,1)S(1)}, bf16[1536,1536]{1,0:T(8,128)(2,1)}, u32[]{:S(2)}) copy-start(bf16[1536,1536]{1,0:T(8,128)(2,1)} %copy-done.1) | copy-start | bytes 14155780
  45.2 1.3 %collective-permute-start.2 = (bf16[128,64]{1,0:T(8,128)(2,1)S(1)}, bf16[128,64]{1,0:T(8,128)(2,1)S(1)}, u32[]{:S(2)}, u32[]{:S(2)}) collective-permute-start(bf16[128,64]{1,0:T(8,128)(2,1)S(1)} %cross_and_compress.1.own_ref), channel_id=1, source_target_pairs={{0,8},{8,0},{1,9},{9,1},{2,10},{10,2},{3,11},{11,3},{4,12},{12,4},... | collective-permute-start | bytes 49160 | tf_op jit(solution)/shard_map/ppermute | solution.py:336

commit v3 on v2

v3 whole, which is shorter than its diff:
```python
import functools
import math

import jax
import jax.numpy as jnp
from jax import lax
from jax.experimental import pallas as pl
from jax.experimental.pallas import tpu as pltpu
from jax.sharding import PartitionSpec as P

LOW = 256
CHUNKS = 4
PAIR = 1
OWN = 5


def arrange_low(table_low, tab, feature):
    embed, vocab = tab.shape[1], tab.shape[2]
    for part in range(0, vocab // LOW, 2):
        pair = [tab[feature, :, pl.ds((part + n) * LOW, LOW)].astype(jnp.float32) for n in range(2)]
        table_low[pl.ds(part * embed, 2 * embed), :] = jnp.concatenate(pair, axis=0).astype(jnp.bfloat16)


def pool_matched(table_low, high, index, between=None):
    rows, bag = index[0].shape[1], len(index)
    embed = table_low.shape[0] // high
    total = None
    for first in range(0, bag, PAIR):
        ids = jnp.concatenate(index[first : first + PAIR], axis=1)
        width = ids.shape[1]
        upper, lower = ids // LOW, ids % LOW
        level = lax.broadcasted_iota(jnp.int32, (LOW, width), 0)
        chosen = (level == lower).astype(jnp.float32).astype(jnp.bfloat16)
        found = jnp.dot(table_low[...], chosen, preferred_element_type=jnp.float32)
        picked = jnp.zeros((embed, width), jnp.float32)
        for part in range(high):
            picked = jnp.where(upper == part, found[part * embed : (part + 1) * embed], picked)
            if between is not None:
                between()
        for j in range(width // rows):
            piece = picked[:, j * rows : (j + 1) * rows]
            total = piece if total is None else total + piece
    return total


def pool_kernel(by_row, tile, groups, row_count, *refs):
    me_ref, ids_hbm, len_hbm, tab_hbm, out_ref, ids_ref, len_ref, shown, tab, table_low, sem = refs[:11]
    features, embed, vocab = tab.shape
    bag, samples = ids_ref.shape[1], ids_ref.shape[2]
    dests = samples // row_count
    high = vocab // LOW
    me = me_ref[0]
    copies = [pltpu.make_async_copy(ids_hbm, ids_ref, sem.at[0]), pltpu.make_async_copy(len_hbm, len_ref, sem.at[1])]
    for copy in copies:
        copy.start()
    parts = []
    if by_row:
        row_ref, pooled, sem_ids = refs[11:14]
        addresses = refs[14:]
        width = vocab // CHUNKS
        for c in range(CHUNKS):
            where = (pl.ds(0, by_row), slice(None), pl.ds(c * width, width))
            parts.append(pltpu.make_async_copy(tab_hbm.at[where], tab.at[where], sem.at[3 + c]))
            parts[-1].start()
    others = pl.ds(by_row, features - by_row)
    rest_copy = pltpu.make_async_copy(tab_hbm.at[others], tab.at[others], sem.at[2])
    rest_copy.start()
    for copy in copies:
        copy.wait()
    for f in range(features):
        for j in range(bag):
            shown[f * bag + j] = jnp.where(j < len_ref[pl.ds(f, 1), :], ids_ref[f, pl.ds(j, 1), :], vocab)
    if by_row:
        moves = [pltpu.make_async_copy(shown.at[n, 0], addresses[n], sem_ids.at[n]) for n in range(by_row * bag)]
        for move in moves:
            move.start()
        row_ref[pl.ds(vocab, 8), :] = jnp.zeros((8, 128), jnp.float32)
        square = [lax.broadcasted_iota(jnp.int32, (LOW, LOW), axis) for axis in range(2)]
        unit = (square[0] == square[1]).astype(jnp.float32).astype(jnp.bfloat16)
        blank = jnp.zeros((128 - by_row * embed, LOW), jnp.float32)

        def build(block, carry, first):
            start = pl.multiple_of(first + block * 2 * LOW, 2 * LOW)
            both = []
            for n in range(2):
                both += [tab[f, :, pl.ds(start + n * LOW, LOW)].astype(jnp.float32) for f in range(by_row)] + [blank]
            columns = jnp.concatenate(both, axis=0).astype(jnp.bfloat16)
            turned = lax.dot_general(unit, columns, (((1,), (1,)), ((), ())), preferred_element_type=jnp.float32)
            row_ref[pl.ds(start, LOW), :] = turned[:, :128]
            row_ref[pl.ds(start + LOW, LOW), :] = turned[:, 128:]
            return carry

        for c in range(CHUNKS):
            parts[c].wait()
            lax.fori_loop(0, width // (2 * LOW), functools.partial(build, first=c * width), 0, unroll=4)
        for move in moves:
            move.wait()
    rest_copy.wait()
    lane = lax.broadcasted_iota(jnp.int32, (1, 128), 1)

    def other(block):
        dest = me + 1 + block
        return jnp.where(dest >= dests, dest - dests, dest)

    def lookups(group):
        eighths = row_count // 8
        row = pl.multiple_of(other(group // eighths) * row_count + group % eighths * 8, 8)
        for u in range(8):
            line = None
            for f in range(by_row):
                found = [row_ref[pl.ds(addresses[f * bag + j][row + u], 1), :] for j in range(bag)]
                total = found[0]
                for item in found[1:]:
                    total = total + item
                line = total if line is None else jnp.where(lane < embed * f, line, total)
                yield
            pooled[pl.ds(row + u, 1), :] = line

    last = (dests - 1) * row_count // 8 - 1
    tiles = samples // tile

    def step(i, carry):
        feature, t = by_row + i // tiles, i % tiles
        pl.when(t == 0)(functools.partial(arrange_low, table_low, tab, feature))
        work = (item for g in range(groups) for item in lookups(jnp.minimum(i * groups + g, last)))
        wanted = groups * 8 * by_row
        count = [0, 0]

        def between():
            count[0] += 1
            while count[1] * (bag // PAIR) * high < count[0] * wanted:
                next(work, None)
                count[1] += 1

        span = pl.ds(pl.multiple_of(t * tile, tile), tile)
        index = [shown[feature * bag + j, :, span] for j in range(bag)]
        total = pool_matched(table_low, high, index, between)
        for block in range(tile // row_count):
            piece = total[:, block * row_count : (block + 1) * row_count]
            out_ref[t * (tile // row_count) + block, feature] = piece.astype(jnp.bfloat16)
        for _ in work:
            pass
        return carry

    steps = (features - by_row) * tiles
    lax.fori_loop(0, steps, step, 0)
    if by_row:

        def rest(group, carry):
            for _ in lookups(group):
                pass
            return carry

        lax.fori_loop(min(steps * groups, last + 1), last + 1, rest, 0)
    if by_row:
        out_ref[me, pl.ds(0, by_row)] = jnp.zeros((by_row, embed, row_count), jnp.bfloat16)

        def finish(block, carry):
            dest = other(block)
            turned = pooled[pl.ds(pl.multiple_of(dest * row_count, row_count), row_count), :].T
            for f in range(by_row):
                out_ref[dest, f] = turned[f * embed : (f + 1) * embed].astype(jnp.bfloat16)
            return carry

        lax.fori_loop(0, dests - 1, finish, 0, unroll=True)


def row_features(features, embed):
    return min(128 // embed, features * 5 // 8)


def pool_features(place, table, ids, lengths, inner_size):
    features, embed, vocab = table.shape
    bag, samples = ids.shape[1], ids.shape[2]
    row_count = samples // inner_size
    tile = row_count * max(1, min(samples, 1024) // row_count)
    by_row = row_features(features, embed)
    steps = (features - by_row) * (samples // tile)
    groups = -(-(samples - row_count) // 8 // steps) if by_row else 0
    hbm = pl.BlockSpec(memory_space=pltpu.HBM)
    scratch = [
        pltpu.VMEM(ids.shape, jnp.int32),
        pltpu.VMEM(lengths.shape, jnp.int32),
        pltpu.VMEM((features * bag, 1, samples), jnp.int32),
        pltpu.VMEM(table.shape, jnp.bfloat16),
        pltpu.VMEM((vocab // LOW * embed, LOW), jnp.bfloat16),
        pltpu.SemaphoreType.DMA((3 + CHUNKS,)),
    ]
    if by_row:
        scratch += [
            pltpu.VMEM((vocab + 8, 128), jnp.float32),
            pltpu.VMEM((samples, 128), jnp.float32),
            pltpu.SemaphoreType.DMA((by_row * bag,)),
        ] + [pltpu.SMEM((samples,), jnp.int32)] * (by_row * bag)
    return pl.pallas_call(
        functools.partial(pool_kernel, by_row, tile, groups, row_count),
        out_shape=pltpu.HBM((inner_size, features, embed, row_count), jnp.bfloat16),
        in_specs=[pl.BlockSpec(memory_space=pltpu.SMEM), hbm, hbm, hbm],
        out_specs=pl.BlockSpec(memory_space=pltpu.VMEM),
        scratch_shapes=scratch,
        compiler_params=pltpu.CompilerParams(vmem_limit_bytes=32 * 2**20),
        name="pool_features",
    )(place, *(pltpu.with_memory_space_constraint(x, pltpu.HBM) for x in (ids, lengths, table)))


def own_kernel(me_ref, ids_ref, len_ref, tab_ref, out_ref, *lows):
    together, vocab = len(lows), tab_ref.shape[2]
    for f, table_low in enumerate(lows):
        arrange_low(table_low, tab_ref, f)
        length = len_ref[pl.ds(pl.program_id(0) * together + f, 1), :]
        index = [jnp.where(j < length, ids_ref[f, pl.ds(j, 1), :], vocab) for j in range(ids_ref.shape[1])]
        out_ref[f] = pool_matched(table_low, vocab // LOW, index).astype(jnp.bfloat16)


def pool_own(place, table, ids, lengths, inner_size):
    all_features, embed, vocab = table.shape
    features = row_features(all_features, embed)
    bag, samples = ids.shape[1], ids.shape[2]
    rows = samples // inner_size
    together = math.gcd(features, OWN)
    return pl.pallas_call(
        own_kernel,
        out_shape=jax.ShapeDtypeStruct((features, embed, rows), jnp.bfloat16),
        grid_spec=pltpu.PrefetchScalarGridSpec(
            num_scalar_prefetch=1,
            grid=(features // together,),
            in_specs=[
                pl.BlockSpec((together, bag, rows), lambda f, me: (f, 0, me[0])),
                pl.BlockSpec((all_features, rows), lambda f, me: (0, me[0])),
                pl.BlockSpec((together, embed, vocab), lambda f, me: (f, 0, 0)),
            ],
            out_specs=pl.BlockSpec((together, embed, rows), lambda f, me: (f, 0, 0)),
            scratch_shapes=[pltpu.VMEM((vocab // LOW * embed, LOW), jnp.bfloat16)] * together,
        ),
        compiler_params=pltpu.CompilerParams(vmem_limit_bytes=16 * 2**20),
        cost_estimate=pl.CostEstimate(
            flops=2 * features * bag * rows * vocab * embed, bytes_accessed=2 * table.size, transcendentals=0
        ),
        name="pool_own",
    )(place, *(pltpu.with_memory_space_constraint(x, pltpu.HBM) for x in (ids, lengths, table)))


def early_kernel(known, tower_ref, other_ref, own_hbm, far_hbm, own_bias_ref, far_bias_ref, gate_ref, *refs):
    early_ref, gate_early_ref, late_ref, gate_late_ref, weights, sem = refs
    tower = tower_ref[0]
    half, experts_in, columns = own_hbm.shape[0], weights.shape[1], weights.shape[2]
    span = pl.ds(pl.multiple_of(tower * columns, columns), columns)
    copies = []
    for n, (source, place) in enumerate([(own_hbm, tower), (far_hbm, 1 - tower)]):
        for e in range(half):
            copies.append(
                pltpu.make_async_copy(source.at[e, :, span], weights.at[place * half + e], sem.at[n * half + e])
            )
            copies[-1].start()
    tasks, experts, depth = gate_ref.shape
    gates = gate_ref[...].astype(jnp.float32).reshape(tasks * experts, depth).astype(jnp.bfloat16)
    gate_early_ref[...] = lax.dot_general(
        other_ref[...], gates[:, :known], (((1,), (1,)), ((), ())), preferred_element_type=jnp.float32
    )
    gate_late_ref[...] = gates[:, known:]
    for n, (bias, place) in enumerate([(own_bias_ref, tower), (far_bias_ref, 1 - tower)]):
        for e in range(half):
            copies[n * half + e].wait()
            at = place * half + e
            found = jnp.dot(other_ref[...], weights[at, pl.ds(0, known), :], preferred_element_type=jnp.float32)
            early_ref[at] = found + bias[pl.ds(e, 1), span]
            late_ref[at] = weights[at, pl.ds(known, experts_in - known), :]


def early_part(tower, other, own_w, far_w, own_b, far_b, gates):
    half, depth, hidden = own_w.shape
    rows, known = other.shape
    columns = hidden // 2
    vmem, hbm = pl.BlockSpec(memory_space=pltpu.VMEM), pl.BlockSpec(memory_space=pltpu.HBM)
    count = gates.shape[0] * gates.shape[1]
    far = lambda x: pltpu.with_memory_space_constraint(x, pltpu.HBM)
    return pl.pallas_call(
        functools.partial(early_kernel, known),
        out_shape=(
            jax.ShapeDtypeStruct((2 * half, rows, columns), jnp.float32),
            jax.ShapeDtypeStruct((rows, count), jnp.float32),
            jax.ShapeDtypeStruct((2 * half, depth - known, columns), jnp.bfloat16),
            jax.ShapeDtypeStruct((count, depth - known), jnp.bfloat16),
        ),
        in_specs=[pl.BlockSpec(memory_space=pltpu.SMEM), vmem, hbm, hbm, vmem, vmem, vmem],
        out_specs=(vmem,) * 4,
        scratch_shapes=[pltpu.VMEM((2 * half, depth, columns), jnp.bfloat16), pltpu.SemaphoreType.DMA((2 * half,))],
        compiler_params=pltpu.CompilerParams(vmem_limit_bytes=16 * 2**20),
        cost_estimate=pl.CostEstimate(
            flops=4 * half * rows * known * columns,
            bytes_accessed=4 * half * depth * columns,
            transcendentals=0,
        ),
        name="early_part",
    )(tower, other, far(own_w), far_w, own_b, far_b, gates)


def cross_kernel(each, by_row, me_ref, slot_ref, rec_ref, own_ref, w_hbm, bias_ref, comp_ref, comp_bias_ref, *refs):
    out_ref, first_t, first, w_ref, sums, sem = refs
    slots, embed, rows = rec_ref.shape
    width, blocks = w_ref.shape[1], sem.shape[0]
    step = width // blocks
    spans = [pl.ds(n * step, step) for n in range(blocks)]
    copies = [pltpu.make_async_copy(w_hbm.at[span], w_ref.at[span], sem.at[n]) for n, span in enumerate(spans)]
    for copy in copies:
        copy.start()
    for f in range(slots):
        first_t[slot_ref[f]] = rec_ref[f].astype(jnp.float32)
    for f in range(by_row):
        first_t[slot_ref[me_ref[0] * each + f]] = own_ref[f].astype(jnp.float32)
    first[...] = first_t[...].reshape(width, rows).T.astype(jnp.bfloat16)
    crossed = bias_ref[...]
    for n, span in enumerate(spans):
        copies[n].wait()
        crossed = crossed + jnp.dot(first[:, span], w_ref[span, :], preferred_element_type=jnp.float32)
        if n + 1 < blocks:
            sums[...] = crossed
            crossed = sums[...]
    total = jnp.zeros((rows, comp_ref.shape[0]), jnp.float32) + comp_bias_ref[...]
    for n, span in enumerate(spans):
        base = first[:, span].astype(jnp.float32)
        second = (base * crossed[:, n * step : (n + 1) * step] + base).astype(jnp.bfloat16)
        total = total + lax.dot_general(
            second, comp_ref[:, span], (((1,), (1,)), ((), ())), preferred_element_type=jnp.float32
        )
    out_ref[...] = total.astype(jnp.bfloat16)


def cross_and_compress(place, slots, received, own, by_row, each, cross_w, cross_b, comp_w, comp_b):
    slot_total, embed, rows = received.shape
    width = cross_w.shape[0]
    vmem, smem = pl.BlockSpec(memory_space=pltpu.VMEM), pl.BlockSpec(memory_space=pltpu.SMEM)
    return pl.pallas_call(
        functools.partial(cross_kernel, each, by_row),
        out_shape=jax.ShapeDtypeStruct((rows, comp_w.shape[1]), jnp.bfloat16),
        in_specs=[smem, smem, vmem, vmem, pl.BlockSpec(memory_space=pltpu.HBM), vmem, vmem, vmem],
        out_specs=vmem,
        scratch_shapes=[
            pltpu.VMEM((slot_total, embed, rows), jnp.float32),
            pltpu.VMEM((rows, width), jnp.bfloat16),
            pltpu.VMEM(cross_w.shape, jnp.bfloat16),
            pltpu.VMEM((rows, width), jnp.float32),
            pltpu.SemaphoreType.DMA((width // 256,)),
        ],
        compiler_params=pltpu.CompilerParams(vmem_limit_bytes=16 * 2**20),
        name="cross_and_compress",
    )(place, slots, received, own, pltpu.with_memory_space_constraint(cross_w, pltpu.HBM), cross_b, comp_w.T, comp_b)


def mix_kernel(tower_ref, early_ref, late_ref, gate_early_ref, gate_late_ref, own_ref, far_ref, out_ref):
    experts, rows, columns = early_ref.shape
    tasks = gate_early_ref.shape[1] // experts
    own, far = own_ref[...], far_ref[...]
    lead = tower_ref[0] == 0
    squeezed = jnp.concatenate([jnp.where(lead, own, far), jnp.where(lead, far, own)], axis=1)
    logits = gate_early_ref[...] + lax.dot_general(
        squeezed, gate_late_ref[...], (((1,), (1,)), ((), ())), preferred_element_type=jnp.float32
    )
    weights = jnp.exp(logits)
    probs = []
    for k in range(tasks):
        mine = weights[:, k * experts : (k + 1) * experts]
        probs.append(mine / jnp.sum(mine, axis=1, keepdims=True))
    totals = [jnp.zeros((rows, columns), jnp.float32) for _ in range(tasks)]
    for e in range(experts):
        hidden = early_ref[e] + jnp.dot(squeezed, late_ref[e], preferred_element_type=jnp.float32)
        hidden = jnp.maximum(hidden, 0.0).astype(jnp.bfloat16).astype(jnp.float32)
        for k in range(tasks):
            totals[k] = totals[k] + probs[k][:, e : e + 1] * hidden
    out_ref[...] = jnp.stack(totals, axis=1).astype(jnp.bfloat16)


def mix_experts(tower, early, late, gate_early, gate_late, own, far):
    experts, rows, columns = early.shape
    tasks = gate_early.shape[1] // experts
    vmem = pl.BlockSpec(memory_space=pltpu.VMEM)
    return pl.pallas_call(
        mix_kernel,
        out_shape=jax.ShapeDtypeStruct((rows, tasks, columns), jnp.bfloat16),
        in_specs=[pl.BlockSpec(memory_space=pltpu.SMEM)] + [vmem] * 6,
        out_specs=vmem,
        compiler_params=pltpu.CompilerParams(vmem_limit_bytes=16 * 2**20),
        name="mix_experts",
    )(tower, early, late, gate_early, gate_late, own, far)


def on_device(
    ids,
    bag_len,
    slot_of_feature,
    tables,
    cross_w,
    cross_b,
    comp_w,
    comp_b,
    other_towers,
    expert_w,
    expert_b,
    gate_w,
):
    inner_size = lax.axis_size("inner")
    tower_size = lax.axis_size("tower")
    tower = lax.axis_index("tower")
    swap = [(n, (n + 1) % tower_size) for n in range(tower_size)]

    far_w = lax.ppermute(expert_w, "tower", swap)
    far_b = lax.ppermute(expert_b, "tower", swap)

    here = lax.axis_index("inner").reshape(1)
    tables_t, ids_t = jnp.transpose(tables[0], (0, 2, 1)), jnp.transpose(ids[0], (0, 2, 1))
    pooled = pool_features(here, tables_t, ids_t, bag_len[0], inner_size)
    dests, features, embed, rows = pooled.shape
    pooled = pooled.reshape(dests, features * embed, rows)
    received = lax.all_to_all(pooled, "inner", split_axis=0, concat_axis=0, tiled=True)
    received = received.reshape(dests * features, embed, rows)

    by_row = row_features(features, embed)
    own = pool_own(here, tables_t, ids_t, bag_len[0], inner_size) if by_row else received[:1]
    place = tower.reshape(1)
    gates = jnp.transpose(gate_w, (1, 2, 0))
    early = early_part(place, other_towers, expert_w, far_w, expert_b, far_b, gates)
    hidden_early, gate_early, late_w, gate_late = early
    received, own, hidden_early = lax.optimization_barrier((received, own, hidden_early))

    squeezed = cross_and_compress(here, slot_of_feature[0], received, own, by_row, features, cross_w[0], cross_b, comp_w[0], comp_b)
    opposite = lax.ppermute(squeezed, "tower", swap)
    return mix_experts(place, hidden_early, late_w, gate_early, gate_late, squeezed, opposite)


def solution(mesh):
    return jax.shard_map(
        on_device,
        mesh=mesh,
        in_specs=(
            P("tower", "inner", "groups", None),
            P("tower", "inner", "groups"),
            P("tower", None),
            P("tower", "inner", None, None),
            P("tower", None, None),
            P("tower", None),
            P("tower", None, None),
            P("tower", None),
            P(("groups", "inner"), None),
            P("tower", None, None),
            P("tower", None),
            P(),
        ),
        out_specs=P(("groups", "inner"), None, "tower"),
        check_vma=False,
    )
```

time: 49.1 us -> 46 us (0.937)
  local copies, waits for them, and re-layouts: 10.7 us -> 0.04 us
  Pallas kernels: 26.8 us -> 34.6 us
    unnamed x26 -> x14, local copies, waits for them, and re-layouts: 10.7 us -> 0.04 us
    pallas_call x2 -> x3, Pallas kernels: 21.5 us -> 28.9 us  [the longest x1 19 us: pool_features(): pl.pallas_call(functools.partial(pool_kernel, by_row, tile, groups, row_c...]
    ppermute x1, waiting for transfers between devices: 1.09 us -> 0.01 us  [on_device(): far_b = lax.ppermute(expert_b, 'tower', swap)]
    all_to_all x1, waiting for transfers between devices: 1.2 us -> 2.05 us  [on_device(): lax.all_to_all(pooled, 'inner', split_axis=0, concat_axis=0, tiled=True)]
  transfers between devices with their start and end apart: 4 -> 4, of which waited for: 3 -> 2; matrix products, arithmetic and copies ran while one was open for 0% -> 0% of each run, Pallas kernels for 46% -> 63%
where the time goes in v3:
time: 46 us; the launch traced here: 45.8 us
  Pallas kernels  34.6 us (75%)
  starting transfers between devices  7.81 us (17%)
  waiting for transfers between devices  3.25 us (7%)
    pallas_call x1, Pallas kernels, pool_features(): pl.pallas_call(functools.partial(pool_kernel, by_row, tile, groups, row_c...  19 us
    all_to_all x1, starting transfers between devices, on_device(): lax.all_to_all(pooled, 'inner', split_axis=0, concat_axis=0, tiled=True)  7 us
    pallas_call x1, Pallas kernels, pool_own(): pl.pallas_call(own_kernel, out_shape=jax.ShapeDtypeStruct((features, embe...  6.41 us
    pallas_call x1, Pallas kernels, cross_and_compress(): pl.pallas_call(functools.partial(cross_kernel, each, by_row), out_shape=j...  3.52 us
    pallas_call x1, Pallas kernels, early_part(): pl.pallas_call(functools.partial(early_kernel, known), out_shape=(jax.Sha...  3.48 us
    pallas_call x1, Pallas kernels, mix_experts(): pl.pallas_call(mix_kernel, out_shape=jax.ShapeDtypeStruct((rows, tasks, c...  2.2 us
    all_to_all x1, waiting for transfers between devices, on_device(): lax.all_to_all(pooled, 'inner', split_axis=0, concat_axis=0, tiled=True)  2.05 us
    ppermute x1, waiting for transfers between devices, on_device(): opposite = lax.ppermute(squeezed, 'tower', swap)  1.19 us
  transfers between devices with their start and end apart: 4, of which 2 were waited for; matrix products, arithmetic and copies ran while one was open for 0% of the time, Pallas kernels for 63%

profile of v3, /device:TPU:0, one launch (start us, length us, event | category | flops | bytes accessed | tf_op | source)
XLA Modules:
  0.0 45.8 jit_solution(16470059764495353139)
XLA Ops:
  0.0 0.0 copy-start.3
  0.0 0.5 collective-permute-start
  0.5 19.0 %pool_features.1 = bf16[8,8,24,128]{3,2,1,0:T(8,128)(2,1)} custom-call(s32[1]{0:T(128)} %bitcast.1.refs_0_.me_ref, s32[8,4,1024]{2,1,0:T(4,128)} %bitcast.25, s32[8,1024]{1,0:T(8,128)} %bitcast.27, bf16[8,24,16384]{2,1,0:T(8,128)(2,1)} %bitcast.21), custom_call_target="tpu_custom_call" | custom-call | tf_op jit(solution)/shard_map/pool_features/pallas_call | solution.py:195
  19.4 0.0 copy-start
  19.5 0.0 copy-start.2
  19.5 7.0 %all-to-all-start = ((bf16[8,192,128]{2,1,0:T(8,128)(2,1)}), bf16[8,192,128]{2,1,0:T(8,128)(2,1)S(1)}, u32[]{:S(2)}, u32[]{:S(2)}) async-start(bf16[8,192,128]{2,1,0:T(8,128)(2,1)} %bitcast.24), calls=%async_computation | async-start | bytes 786432 | tf_op jit(solution)/shard_map/all_to_all | solution.py:414
  26.5 0.0 copy-done.3
  26.5 0.3 collective-permute-start.1
  26.8 6.4 %pool_own.1.own_ref = bf16[5,24,128]{2,1,0:T(8,128)(2,1)S(1)} custom-call(s32[1]{0:T(128)} %bitcast.1.refs_0_.me_ref, s32[8,4,1024]{2,1,0:T(4,128)} %bitcast.26, s32[8,1024]{1,0:T(8,128)} %bitcast.28, bf16[8,24,16384]{2,1,0:T(8,128)(2,1)} %bitcast.22), custom_call_target="tpu_custom_call" | custom-call | flops 2013265920 | bytes 6291456 | tf_op jit(solution)/shard_map/pool_own/pallas_call | solution.py:221
  33.2 0.0 copy-start.1
  33.2 0.0 copy-start.4
  33.2 0.0 copy-start.5
  33.2 0.0 copy-start.6
  33.2 0.0 collective-permute-done.1.far_bias_ref
  33.2 0.0 collective-permute-done.far_hbm
  33.3 0.0 copy-done
  33.3 0.0 copy-done.2
  33.3 3.5 %early_part.1 = (f32[8,128,256]{2,1,0:T(8,128)S(1)}, f32[128,32]{1,0:T(8,128)S(1)}, bf16[8,128,256]{2,1,0:T(8,128)(2,1)S(1)}, bf16[32,128]{1,0:T(8,128)(2,1)S(1)}) custom-call(s32[1]{0:T(128)} %bitcast.tower_ref, bf16[128,896]{1,0:T(8,128)(2,1)S(1)} %copy-done, bf16[4,1024,512]{2,1,0:T(8,128)(2,1)} %own_hbm.1, ...), custom_call_target="tpu_custom_call" | custom-call | flops 469762048 | bytes 4194304 | tf_op jit(solution)/shard_map/early_part/pallas_call | solution.py:277
  36.8 2.1 %all-to-all-done = bf16[8,192,128]{2,1,0:T(8,128)(2,1)S(1)} async-done(((bf16[8,192,128]{2,1,0:T(8,128)(2,1)}), bf16[8,192,128]{2,1,0:T(8,128)(2,1)S(1)}, u32[]{:S(2)}, u32[]{:S(2)}) %all-to-all-start) | async-done | bytes 393248 | tf_op jit(solution)/shard_map/all_to_all | solution.py:414
  38.8 0.0 copy-done.1
  38.8 0.0 copy-done.4
  38.8 0.0 copy-done.5
  38.8 0.0 copy-done.6
  38.8 3.5 %cross_and_compress.1.own_ref = bf16[128,64]{1,0:T(8,128)(2,1)S(1)} custom-call(s32[1]{0:T(128)} %bitcast.1.refs_0_.me_ref, s32[64]{0:T(128)S(1)} %bitcast.20, bf16[64,24,128]{2,1,0:T(8,128)(2,1)S(1)} %bitcast.17, bf16[5,24,128]{2,1,0:T(8,128)(2,1)S(1)} %pool_own.1.own_ref, bf16[1536,1536]{1,0:T(8,128)(2,1)} %bitcast.23, f32[1,1536]{1,0:T(1,128)S(1)} %copy-done.4, ...), custom_call_target="tpu_custom_call" | custom-call | tf_op jit(solution)/shard_map/cross_and_compress/pallas_call | solution.py:333
  42.4 0.1 collective-permute-start.2
  42.4 1.2 %collective-permute-done.2.far_ref = bf16[128,64]{1,0:T(8,128)(2,1)S(1)} collective-permute-done((bf16[128,64]{1,0:T(8,128)(2,1)S(1)}, bf16[128,64]{1,0:T(8,128)(2,1)S(1)}, u32[]{:S(2)}, u32[]{:S(2)}) %collective-permute-start.2) | collective-permute-done | bytes 16416 | tf_op jit(solution)/shard_map/ppermute | solution.py:426
  43.6 2.2 %mix_experts.1 = bf16[128,4,256]{2,1,0:T(4,128)(2,1)} custom-call(s32[1]{0:T(128)} %bitcast.tower_ref, f32[8,128,256]{2,1,0:T(8,128)S(1)} %get-tuple-element.13.early_ref, bf16[8,128,256]{2,1,0:T(8,128)(2,1)S(1)} %get-tuple-element.14.late_ref, f32[128,32]{1,0:T(8,128)S(1)} %get-tuple-element.15.gate_early_ref, ...), custom_call_target="tpu_custom_call" | custom-call | tf_op jit(solution)/shard_map/mix_experts/pallas_call | solution.py:377
Async XLA Ops:
  0.0 26.5 %copy-start.3 = (f32[4,512]{1,0:T(4,128)S(1)}, f32[4,512]{1,0:T(4,128)}, u32[]{:S(2)}) copy-start(f32[4,512]{1,0:T(4,128)} %own_bias_ref.1) | copy-start | bytes 24580
  0.0 33.2 %collective-permute-start = (bf16[4,1024,512]{2,1,0:T(8,128)(2,1)}, bf16[4,1024,512]{2,1,0:T(8,128)(2,1)}, u32[]{:S(2)}, u32[]{:S(2)}) collective-permute-start(bf16[4,1024,512]{2,1,0:T(8,128)(2,1)} %own_hbm.1), channel_id=1, source_target_pairs={{0,8},{8,0},{1,9},{9,1},{2,10},{10,2},{3,11},{11,3},{4,12},{12,4},... | collective-permute-start | bytes 12582920 | tf_op jit(solution)/shard_map/ppermute | solution.py:406
  19.4 13.8 %copy-start = (bf16[128,896]{1,0:T(8,128)(2,1)S(1)}, bf16[128,896]{1,0:T(8,128)(2,1)}, u32[]{:S(2)}) copy-start(bf16[128,896]{1,0:T(8,128)(2,1)} %other_ref.1) | copy-start | bytes 688132
  19.5 13.8 %copy-start.2 = (bf16[1024,4,8]{0,2,1:T(8,128)(2,1)S(1)}, bf16[1024,4,8]{0,2,1:T(8,128)(2,1)}, u32[]{:S(2)}) copy-start(bf16[1024,4,8]{0,2,1:T(8,128)(2,1)} %param.23) | copy-start | bytes 196612
  19.5 19.3 %all-to-all-start = ((bf16[8,192,128]{2,1,0:T(8,128)(2,1)}), bf16[8,192,128]{2,1,0:T(8,128)(2,1)S(1)}, u32[]{:S(2)}, u32[]{:S(2)}) async-start(bf16[8,192,128]{2,1,0:T(8,128)(2,1)} %bitcast.24), calls=%async_computation | async-start | bytes 786432 | tf_op jit(solution)/shard_map/all_to_all | solution.py:414
  26.5 6.8 %collective-permute-start.1 = (f32[4,512]{1,0:T(4,128)S(1)}, f32[4,512]{1,0:T(4,128)S(1)}, u32[]{:S(2)}, u32[]{:S(2)}) collective-permute-start(f32[4,512]{1,0:T(4,128)S(1)} %copy-done.3), channel_id=1, source_target_pairs={{0,8},{8,0},{1,9},{9,1},{2,10},{10,2},{3,11},{11,3},{4,12},{12,4},... | collective-permute-start | bytes 24584 | tf_op jit(solution)/shard_map/ppermute | solution.py:407
  33.2 5.6 %copy-start.1 = (bf16[1,1536,64]{1,2,0:T(8,128)(2,1)S(1)}, bf16[1,1536,64]{1,2,0:T(8,128)(2,1)}, u32[]{:S(2)}) copy-start(bf16[1,1536,64]{1,2,0:T(8,128)(2,1)} %param.18) | copy-start | bytes 589828
  33.2 5.6 %copy-start.4 = (f32[1,1536]{1,0:T(1,128)S(1)}, f32[1,1536]{1,0:T(1,128)}, u32[]{:S(2)}) copy-start(f32[1,1536]{1,0:T(1,128)} %bias_ref.1) | copy-start | bytes 18436
  33.2 5.6 %copy-start.5 = (s32[1,64]{1,0:T(1,128)S(1)}, s32[1,64]{1,0:T(1,128)}, u32[]{:S(2)}) copy-start(s32[1,64]{1,0:T(1,128)} %param.14) | copy-start | bytes 772
  33.2 5.6 %copy-start.6 = (f32[1,64]{1,0:T(1,128)S(1)}, f32[1,64]{1,0:T(1,128)}, u32[]{:S(2)}) copy-start(f32[1,64]{1,0:T(1,128)} %comp_bias_ref.1) | copy-start | bytes 772
  42.4 1.3 %collective-permute-start.2 = (bf16[128,64]{1,0:T(8,128)(2,1)S(1)}, bf16[128,64]{1,0:T(8,128)(2,1)S(1)}, u32[]{:S(2)}, u32[]{:S(2)}) collective-permute-start(bf16[128,64]{1,0:T(8,128)(2,1)S(1)} %cross_and_compress.1.own_ref), channel_id=1, source_target_pairs={{0,8},{8,0},{1,9},{9,1},{2,10},{10,2},{3,11},{11,3},{4,12},{12,4},... | collective-permute-start | bytes 49160 | tf_op jit(solution)/shard_map/ppermute | solution.py:426

commit v4 on v3

--- a/solution.py
+++ b/solution.py
@@ -9,7 +9,8 @@
 from jax.sharding import PartitionSpec as P
 
 LOW = 256
-CHUNKS = 4
+SHIFT = 8
+CHUNKS = 8
 PAIR = 1
 OWN = 5
 
@@ -28,7 +29,7 @@
     for first in range(0, bag, PAIR):
         ids = jnp.concatenate(index[first : first + PAIR], axis=1)
         width = ids.shape[1]
-        upper, lower = ids // LOW, ids % LOW
+        upper, lower = jnp.broadcast_to(ids >> SHIFT, (embed, width)), ids & (LOW - 1)
         level = lax.broadcasted_iota(jnp.int32, (LOW, width), 0)
         chosen = (level == lower).astype(jnp.float32).astype(jnp.bfloat16)
         found = jnp.dot(table_low[...], chosen, preferred_element_type=jnp.float32)
@@ -64,7 +65,8 @@
             parts[-1].start()
     others = pl.ds(by_row, features - by_row)
     rest_copy = pltpu.make_async_copy(tab_hbm.at[others], tab.at[others], sem.at[2])
-    rest_copy.start()
+    if not by_row:
+        rest_copy.start()
     for copy in copies:
         copy.wait()
     for f in range(features):
@@ -92,6 +94,8 @@
 
         for c in range(CHUNKS):
             parts[c].wait()
+            if c == CHUNKS // 2 - 1:
+                rest_copy.start()
             lax.fori_loop(0, width // (2 * LOW), functools.partial(build, first=c * width), 0, unroll=4)
         for move in moves:
             move.wait()
@@ -176,7 +180,7 @@
     tile = row_count * max(1, min(samples, 1024) // row_count)
     by_row = row_features(features, embed)
     steps = (features - by_row) * (samples // tile)
-    groups = -(-(samples - row_count) // 8 // steps) if by_row else 0
+    groups = (samples - row_count) // 8 // steps if by_row else 0
     hbm = pl.BlockSpec(memory_space=pltpu.HBM)
     scratch = [
         pltpu.VMEM(ids.shape, jnp.int32),
@@ -347,7 +351,7 @@
     )(place, slots, received, own, pltpu.with_memory_space_constraint(cross_w, pltpu.HBM), cross_b, comp_w.T, comp_b)
 
 
-def mix_kernel(tower_ref, early_ref, late_ref, gate_early_ref, gate_late_ref, own_ref, far_ref, out_ref):
+def mix_kernel(tower_ref, early_ref, late_ref, gate_early_ref, gate_late_ref, own_ref, far_ref, out_ref, hidden_ref, lines_ref):
     experts, rows, columns = early_ref.shape
     tasks = gate_early_ref.shape[1] // experts
     own, far = own_ref[...], far_ref[...]
@@ -361,13 +365,21 @@
     for k in range(tasks):
         mine = weights[:, k * experts : (k + 1) * experts]
         probs.append(mine / jnp.sum(mine, axis=1, keepdims=True))
-    totals = [jnp.zeros((rows, columns), jnp.float32) for _ in range(tasks)]
     for e in range(experts):
         hidden = early_ref[e] + jnp.dot(squeezed, late_ref[e], preferred_element_type=jnp.float32)
-        hidden = jnp.maximum(hidden, 0.0).astype(jnp.bfloat16).astype(jnp.float32)
-        for k in range(tasks):
-            totals[k] = totals[k] + probs[k][:, e : e + 1] * hidden
-    out_ref[...] = jnp.stack(totals, axis=1).astype(jnp.bfloat16)
+        hidden_ref[e] = jnp.maximum(hidden, 0.0).astype(jnp.bfloat16).astype(jnp.float32)
+    step = math.gcd(rows, 32)
+    for first in range(0, rows, step):
+        totals = [0.0] * tasks
+        for e in range(experts):
+            hidden = hidden_ref[e, pl.ds(first, step), :]
+            for k in range(tasks):
+                totals[k] = totals[k] + probs[k][first : first + step, e : e + 1] * hidden
+        for c in range(columns // 128):
+            for k in range(tasks):
+                lines_ref[c, pl.ds(first * tasks + k, step, stride=tasks), :] = totals[k][:, c * 128 : (c + 1) * 128]
+            lines = lines_ref[c, pl.ds(first * tasks, step * tasks), :].reshape(step, tasks, 128)
+            out_ref[pl.ds(first, step), :, pl.ds(c * 128, 128)] = lines.astype(jnp.bfloat16)
 
 
 def mix_experts(tower, early, late, gate_early, gate_late, own, far):
@@ -379,6 +391,10 @@
         out_shape=jax.ShapeDtypeStruct((rows, tasks, columns), jnp.bfloat16),
         in_specs=[pl.BlockSpec(memory_space=pltpu.SMEM)] + [vmem] * 6,
         out_specs=vmem,
+        scratch_shapes=[
+            pltpu.VMEM((experts, rows, columns), jnp.float32),
+            pltpu.VMEM((columns // 128, rows * tasks, 128), jnp.float32),
+        ],
         compiler_params=pltpu.CompilerParams(vmem_limit_bytes=16 * 2**20),
         name="mix_experts",
     )(tower, early, late, gate_early, gate_late, own, far)

time: 46 us -> 44.6 us (0.970)
  Pallas kernels: 34.6 us -> 33.2 us
    pallas_call x1, Pallas kernels: 19 us -> 17.7 us  [pool_features(): pl.pallas_call(functools.partial(pool_kernel, by_row, tile, groups, row_c...]
  transfers between devices with their start and end apart: 4 -> 4, of which waited for: 2 -> 2; matrix products, arithmetic and copies ran while one was open for 0% -> 0% of each run, Pallas kernels for 63% -> 62%
where the time goes in v4:
time: 44.6 us; the launch traced here: 44.4 us
  Pallas kernels  33.2 us (74%)
  starting transfers between devices  7.81 us (18%)
  waiting for transfers between devices  3.26 us (7%)
    pallas_call x1, Pallas kernels, pool_features(): pl.pallas_call(functools.partial(pool_kernel, by_row, tile, groups, row_c...  17.7 us
    all_to_all x1, starting transfers between devices, on_device(): lax.all_to_all(pooled, 'inner', split_axis=0, concat_axis=0, tiled=True)  6.96 us
    pallas_call x1, Pallas kernels, pool_own(): pl.pallas_call(own_kernel, out_shape=jax.ShapeDtypeStruct((features, embe...  6.41 us
    pallas_call x1, Pallas kernels, cross_and_compress(): pl.pallas_call(functools.partial(cross_kernel, each, by_row), out_shape=j...  3.52 us
    pallas_call x1, Pallas kernels, early_part(): pl.pallas_call(functools.partial(early_kernel, known), out_shape=(jax.Sha...  3.48 us
    pallas_call x1, Pallas kernels, mix_experts(): pl.pallas_call(mix_kernel, out_shape=jax.ShapeDtypeStruct((rows, tasks, c...  2.08 us
    all_to_all x1, waiting for transfers between devices, on_device(): lax.all_to_all(pooled, 'inner', split_axis=0, concat_axis=0, tiled=True)  2.06 us
    ppermute x1, waiting for transfers between devices, on_device(): opposite = lax.ppermute(squeezed, 'tower', swap)  1.19 us
  transfers between devices with their start and end apart: 4, of which 2 were waited for; matrix products, arithmetic and copies ran while one was open for 0% of the time, Pallas kernels for 62%

profile of v4, /device:TPU:0, one launch (start us, length us, event | category | flops | bytes accessed | tf_op | source)
XLA Modules:
  0.0 44.4 jit_solution(14951371704919796870)
XLA Ops:
  0.0 0.0 copy-start.3
  0.0 0.5 %collective-permute-start = (bf16[4,1024,512]{2,1,0:T(8,128)(2,1)}, bf16[4,1024,512]{2,1,0:T(8,128)(2,1)}, u32[]{:S(2)}, u32[]{:S(2)}) collective-permute-start(bf16[4,1024,512]{2,1,0:T(8,128)(2,1)} %own_hbm.1), channel_id=1, source_target_pairs={{0,8},{8,0},{1,9},{9,1},{2,10},{10,2},{3,11},{11,3},{4,12},{12,4},... | collective-permute-start | bytes 12582920 | tf_op jit(solution)/shard_map/ppermute | solution.py:422
  0.5 17.7 %pool_features.1 = bf16[8,8,24,128]{3,2,1,0:T(8,128)(2,1)} custom-call(s32[1]{0:T(128)} %bitcast.1.refs_0_.me_ref, s32[8,4,1024]{2,1,0:T(4,128)} %bitcast.25, s32[8,1024]{1,0:T(8,128)} %bitcast.27, bf16[8,24,16384]{2,1,0:T(8,128)(2,1)} %bitcast.21), custom_call_target="tpu_custom_call" | custom-call | tf_op jit(solution)/shard_map/pool_features/pallas_call | solution.py:199
  18.1 0.0 copy-start
  18.2 0.0 copy-start.2
  18.2 7.0 %all-to-all-start = ((bf16[8,192,128]{2,1,0:T(8,128)(2,1)}), bf16[8,192,128]{2,1,0:T(8,128)(2,1)S(1)}, u32[]{:S(2)}, u32[]{:S(2)}) async-start(bf16[8,192,128]{2,1,0:T(8,128)(2,1)} %bitcast.24), calls=%async_computation | async-start | bytes 786432 | tf_op jit(solution)/shard_map/all_to_all | solution.py:430
  25.1 0.0 copy-done.3
  25.1 0.3 collective-permute-start.1
  25.5 6.4 %pool_own.1.own_ref = bf16[5,24,128]{2,1,0:T(8,128)(2,1)S(1)} custom-call(s32[1]{0:T(128)} %bitcast.1.refs_0_.me_ref, s32[8,4,1024]{2,1,0:T(4,128)} %bitcast.26, s32[8,1024]{1,0:T(8,128)} %bitcast.28, bf16[8,24,16384]{2,1,0:T(8,128)(2,1)} %bitcast.22), custom_call_target="tpu_custom_call" | custom-call | flops 2013265920 | bytes 6291456 | tf_op jit(solution)/shard_map/pool_own/pallas_call | solution.py:225
  31.9 0.0 copy-start.1
  31.9 0.0 copy-start.4
  31.9 0.0 copy-start.5
  31.9 0.0 copy-start.6
  31.9 0.0 collective-permute-done.1.far_bias_ref
  31.9 0.0 collective-permute-done.far_hbm
  32.0 0.0 copy-done
  32.0 0.0 copy-done.2
  32.0 3.5 %early_part.1 = (f32[8,128,256]{2,1,0:T(8,128)S(1)}, f32[128,32]{1,0:T(8,128)S(1)}, bf16[8,128,256]{2,1,0:T(8,128)(2,1)S(1)}, bf16[32,128]{1,0:T(8,128)(2,1)S(1)}) custom-call(s32[1]{0:T(128)} %bitcast.tower_ref, bf16[128,896]{1,0:T(8,128)(2,1)S(1)} %copy-done, bf16[4,1024,512]{2,1,0:T(8,128)(2,1)} %own_hbm.1, ...), custom_call_target="tpu_custom_call" | custom-call | flops 469762048 | bytes 4194304 | tf_op jit(solution)/shard_map/early_part/pallas_call | solution.py:281
  35.5 2.1 %all-to-all-done = bf16[8,192,128]{2,1,0:T(8,128)(2,1)S(1)} async-done(((bf16[8,192,128]{2,1,0:T(8,128)(2,1)}), bf16[8,192,128]{2,1,0:T(8,128)(2,1)S(1)}, u32[]{:S(2)}, u32[]{:S(2)}) %all-to-all-start) | async-done | bytes 393248 | tf_op jit(solution)/shard_map/all_to_all | solution.py:430
  37.5 0.0 copy-done.1
  37.5 0.0 copy-done.4
  37.5 0.0 copy-done.5
  37.5 0.0 copy-done.6
  37.5 3.5 %cross_and_compress.1.own_ref = bf16[128,64]{1,0:T(8,128)(2,1)S(1)} custom-call(s32[1]{0:T(128)} %bitcast.1.refs_0_.me_ref, s32[64]{0:T(128)S(1)} %bitcast.20, bf16[64,24,128]{2,1,0:T(8,128)(2,1)S(1)} %bitcast.17, bf16[5,24,128]{2,1,0:T(8,128)(2,1)S(1)} %pool_own.1.own_ref, bf16[1536,1536]{1,0:T(8,128)(2,1)} %bitcast.23, f32[1,1536]{1,0:T(1,128)S(1)} %copy-done.4, ...), custom_call_target="tpu_custom_call" | custom-call | tf_op jit(solution)/shard_map/cross_and_compress/pallas_call | solution.py:337
  41.1 0.1 collective-permute-start.2
  41.1 1.2 %collective-permute-done.2.far_ref = bf16[128,64]{1,0:T(8,128)(2,1)S(1)} collective-permute-done((bf16[128,64]{1,0:T(8,128)(2,1)S(1)}, bf16[128,64]{1,0:T(8,128)(2,1)S(1)}, u32[]{:S(2)}, u32[]{:S(2)}) %collective-permute-start.2) | collective-permute-done | bytes 16416 | tf_op jit(solution)/shard_map/ppermute | solution.py:442
  42.3 2.1 %mix_experts.1 = bf16[128,4,256]{2,1,0:T(4,128)(2,1)} custom-call(s32[1]{0:T(128)} %bitcast.tower_ref, f32[8,128,256]{2,1,0:T(8,128)S(1)} %get-tuple-element.13.early_ref, bf16[8,128,256]{2,1,0:T(8,128)(2,1)S(1)} %get-tuple-element.14.late_ref, f32[128,32]{1,0:T(8,128)S(1)} %get-tuple-element.15.gate_early_ref, ...), custom_call_target="tpu_custom_call" | custom-call | tf_op jit(solution)/shard_map/mix_experts/pallas_call | solution.py:389
Async XLA Ops:
  0.0 25.1 %copy-start.3 = (f32[4,512]{1,0:T(4,128)S(1)}, f32[4,512]{1,0:T(4,128)}, u32[]{:S(2)}) copy-start(f32[4,512]{1,0:T(4,128)} %own_bias_ref.1) | copy-start | bytes 24580
  0.0 31.9 %collective-permute-start = (bf16[4,1024,512]{2,1,0:T(8,128)(2,1)}, bf16[4,1024,512]{2,1,0:T(8,128)(2,1)}, u32[]{:S(2)}, u32[]{:S(2)}) collective-permute-start(bf16[4,1024,512]{2,1,0:T(8,128)(2,1)} %own_hbm.1), channel_id=1, source_target_pairs={{0,8},{8,0},{1,9},{9,1},{2,10},{10,2},{3,11},{11,3},{4,12},{12,4},... | collective-permute-start | bytes 12582920 | tf_op jit(solution)/shard_map/ppermute | solution.py:422
  18.1 13.8 %copy-start = (bf16[128,896]{1,0:T(8,128)(2,1)S(1)}, bf16[128,896]{1,0:T(8,128)(2,1)}, u32[]{:S(2)}) copy-start(bf16[128,896]{1,0:T(8,128)(2,1)} %other_ref.1) | copy-start | bytes 688132
  18.2 13.8 %copy-start.2 = (bf16[1024,4,8]{0,2,1:T(8,128)(2,1)S(1)}, bf16[1024,4,8]{0,2,1:T(8,128)(2,1)}, u32[]{:S(2)}) copy-start(bf16[1024,4,8]{0,2,1:T(8,128)(2,1)} %param.23) | copy-start | bytes 196612
  18.2 19.3 %all-to-all-start = ((bf16[8,192,128]{2,1,0:T(8,128)(2,1)}), bf16[8,192,128]{2,1,0:T(8,128)(2,1)S(1)}, u32[]{:S(2)}, u32[]{:S(2)}) async-start(bf16[8,192,128]{2,1,0:T(8,128)(2,1)} %bitcast.24), calls=%async_computation | async-start | bytes 786432 | tf_op jit(solution)/shard_map/all_to_all | solution.py:430
  25.1 6.8 %collective-permute-start.1 = (f32[4,512]{1,0:T(4,128)S(1)}, f32[4,512]{1,0:T(4,128)S(1)}, u32[]{:S(2)}, u32[]{:S(2)}) collective-permute-start(f32[4,512]{1,0:T(4,128)S(1)} %copy-done.3), channel_id=1, source_target_pairs={{0,8},{8,0},{1,9},{9,1},{2,10},{10,2},{3,11},{11,3},{4,12},{12,4},... | collective-permute-start | bytes 24584 | tf_op jit(solution)/shard_map/ppermute | solution.py:423
  31.9 5.6 %copy-start.1 = (bf16[1,1536,64]{1,2,0:T(8,128)(2,1)S(1)}, bf16[1,1536,64]{1,2,0:T(8,128)(2,1)}, u32[]{:S(2)}) copy-start(bf16[1,1536,64]{1,2,0:T(8,128)(2,1)} %param.18) | copy-start | bytes 589828
  31.9 5.6 %copy-start.4 = (f32[1,1536]{1,0:T(1,128)S(1)}, f32[1,1536]{1,0:T(1,128)}, u32[]{:S(2)}) copy-start(f32[1,1536]{1,0:T(1,128)} %bias_ref.1) | copy-start | bytes 18436
  31.9 5.6 %copy-start.5 = (s32[1,64]{1,0:T(1,128)S(1)}, s32[1,64]{1,0:T(1,128)}, u32[]{:S(2)}) copy-start(s32[1,64]{1,0:T(1,128)} %param.14) | copy-start | bytes 772
  31.9 5.6 %copy-start.6 = (f32[1,64]{1,0:T(1,128)S(1)}, f32[1,64]{1,0:T(1,128)}, u32[]{:S(2)}) copy-start(f32[1,64]{1,0:T(1,128)} %comp_bias_ref.1) | copy-start | bytes 772
  41.1 1.3 %collective-permute-start.2 = (bf16[128,64]{1,0:T(8,128)(2,1)S(1)}, bf16[128,64]{1,0:T(8,128)(2,1)S(1)}, u32[]{:S(2)}, u32[]{:S(2)}) collective-permute-start(bf16[128,64]{1,0:T(8,128)(2,1)S(1)} %cross_and_compress.1.own_ref), channel_id=1, source_target_pairs={{0,8},{8,0},{1,9},{9,1},{2,10},{10,2},{3,11},{11,3},{4,12},{12,4},... | collective-permute-start | bytes 49160 | tf_op jit(solution)/shard_map/ppermute | solution.py:442

commit v5 on v4

--- a/solution.py
+++ b/solution.py
@@ -10,7 +10,7 @@
 
 LOW = 256
 SHIFT = 8
-CHUNKS = 8
+CHUNKS = 4
 PAIR = 1
 OWN = 5
 
@@ -96,7 +96,7 @@
             parts[c].wait()
             if c == CHUNKS // 2 - 1:
                 rest_copy.start()
-            lax.fori_loop(0, width // (2 * LOW), functools.partial(build, first=c * width), 0, unroll=4)
+            lax.fori_loop(0, width // (2 * LOW), functools.partial(build, first=c * width), 0, unroll=8)
         for move in moves:
             move.wait()
     rest_copy.wait()

time: 44.6 us -> 44.2 us (level)
  Pallas kernels: 33.2 us -> 32.7 us
    pallas_call x1, Pallas kernels: 17.7 us -> 17.2 us  [pool_features(): pl.pallas_call(functools.partial(pool_kernel, by_row, tile, groups, row_c...]
where the time goes in v5:
time: 44.2 us; the launch traced here: 44 us
  Pallas kernels  32.7 us (74%)
  starting transfers between devices  7.83 us (18%)
  waiting for transfers between devices  3.26 us (7%)
    pallas_call x1, Pallas kernels, pool_features(): pl.pallas_call(functools.partial(pool_kernel, by_row, tile, groups, row_c...  17.2 us
    all_to_all x1, starting transfers between devices, on_device(): lax.all_to_all(pooled, 'inner', split_axis=0, concat_axis=0, tiled=True)  7 us
    pallas_call x1, Pallas kernels, pool_own(): pl.pallas_call(own_kernel, out_shape=jax.ShapeDtypeStruct((features, embe...  6.41 us
    pallas_call x1, Pallas kernels, cross_and_compress(): pl.pallas_call(functools.partial(cross_kernel, each, by_row), out_shape=j...  3.52 us
    pallas_call x1, Pallas kernels, early_part(): pl.pallas_call(functools.partial(early_kernel, known), out_shape=(jax.Sha...  3.48 us
    pallas_call x1, Pallas kernels, mix_experts(): pl.pallas_call(mix_kernel, out_shape=jax.ShapeDtypeStruct((rows, tasks, c...  2.08 us
    all_to_all x1, waiting for transfers between devices, on_device(): lax.all_to_all(pooled, 'inner', split_axis=0, concat_axis=0, tiled=True)  2.06 us
    ppermute x1, waiting for transfers between devices, on_device(): opposite = lax.ppermute(squeezed, 'tower', swap)  1.19 us
  transfers between devices with their start and end apart: 4, of which 2 were waited for; matrix products, arithmetic and copies ran while one was open for 0% of the time, Pallas kernels for 62%

profile of v5, /device:TPU:0, one launch (start us, length us, event | category | flops | bytes accessed | tf_op | source)
XLA Modules:
  0.0 44.0 jit_solution(11162026904381937068)
XLA Ops:
  0.0 0.0 copy-start.3
  0.0 0.5 %collective-permute-start = (bf16[4,1024,512]{2,1,0:T(8,128)(2,1)}, bf16[4,1024,512]{2,1,0:T(8,128)(2,1)}, u32[]{:S(2)}, u32[]{:S(2)}) collective-permute-start(bf16[4,1024,512]{2,1,0:T(8,128)(2,1)} %own_hbm.1), channel_id=1, source_target_pairs={{0,8},{8,0},{1,9},{9,1},{2,10},{10,2},{3,11},{11,3},{4,12},{12,4},... | collective-permute-start | bytes 12582920 | tf_op jit(solution)/shard_map/ppermute | solution.py:422
  0.5 17.2 %pool_features.1 = bf16[8,8,24,128]{3,2,1,0:T(8,128)(2,1)} custom-call(s32[1]{0:T(128)} %bitcast.1.refs_0_.me_ref, s32[8,4,1024]{2,1,0:T(4,128)} %bitcast.25, s32[8,1024]{1,0:T(8,128)} %bitcast.27, bf16[8,24,16384]{2,1,0:T(8,128)(2,1)} %bitcast.21), custom_call_target="tpu_custom_call" | custom-call | tf_op jit(solution)/shard_map/pool_features/pallas_call | solution.py:199
  17.7 0.0 copy-start
  17.7 0.0 copy-start.2
  17.7 7.0 %all-to-all-start = ((bf16[8,192,128]{2,1,0:T(8,128)(2,1)}), bf16[8,192,128]{2,1,0:T(8,128)(2,1)S(1)}, u32[]{:S(2)}, u32[]{:S(2)}) async-start(bf16[8,192,128]{2,1,0:T(8,128)(2,1)} %bitcast.24), calls=%async_computation | async-start | bytes 786432 | tf_op jit(solution)/shard_map/all_to_all | solution.py:430
  24.7 0.0 copy-done.3
  24.7 0.3 collective-permute-start.1
  25.0 6.4 %pool_own.1.own_ref = bf16[5,24,128]{2,1,0:T(8,128)(2,1)S(1)} custom-call(s32[1]{0:T(128)} %bitcast.1.refs_0_.me_ref, s32[8,4,1024]{2,1,0:T(4,128)} %bitcast.26, s32[8,1024]{1,0:T(8,128)} %bitcast.28, bf16[8,24,16384]{2,1,0:T(8,128)(2,1)} %bitcast.22), custom_call_target="tpu_custom_call" | custom-call | flops 2013265920 | bytes 6291456 | tf_op jit(solution)/shard_map/pool_own/pallas_call | solution.py:225
  31.4 0.0 copy-start.1
  31.4 0.0 copy-start.4
  31.4 0.0 copy-start.5
  31.5 0.0 copy-start.6
  31.5 0.0 collective-permute-done.1.far_bias_ref
  31.5 0.0 collective-permute-done.far_hbm
  31.5 0.0 copy-done
  31.5 0.0 copy-done.2
  31.5 3.5 %early_part.1 = (f32[8,128,256]{2,1,0:T(8,128)S(1)}, f32[128,32]{1,0:T(8,128)S(1)}, bf16[8,128,256]{2,1,0:T(8,128)(2,1)S(1)}, bf16[32,128]{1,0:T(8,128)(2,1)S(1)}) custom-call(s32[1]{0:T(128)} %bitcast.tower_ref, bf16[128,896]{1,0:T(8,128)(2,1)S(1)} %copy-done, bf16[4,1024,512]{2,1,0:T(8,128)(2,1)} %own_hbm.1, ...), custom_call_target="tpu_custom_call" | custom-call | flops 469762048 | bytes 4194304 | tf_op jit(solution)/shard_map/early_part/pallas_call | solution.py:281
  35.0 2.1 %all-to-all-done = bf16[8,192,128]{2,1,0:T(8,128)(2,1)S(1)} async-done(((bf16[8,192,128]{2,1,0:T(8,128)(2,1)}), bf16[8,192,128]{2,1,0:T(8,128)(2,1)S(1)}, u32[]{:S(2)}, u32[]{:S(2)}) %all-to-all-start) | async-done | bytes 393248 | tf_op jit(solution)/shard_map/all_to_all | solution.py:430
  37.1 0.0 copy-done.1
  37.1 0.0 copy-done.4
  37.1 0.0 copy-done.5
  37.1 0.0 copy-done.6
  37.1 3.5 %cross_and_compress.1.own_ref = bf16[128,64]{1,0:T(8,128)(2,1)S(1)} custom-call(s32[1]{0:T(128)} %bitcast.1.refs_0_.me_ref, s32[64]{0:T(128)S(1)} %bitcast.20, bf16[64,24,128]{2,1,0:T(8,128)(2,1)S(1)} %bitcast.17, bf16[5,24,128]{2,1,0:T(8,128)(2,1)S(1)} %pool_own.1.own_ref, bf16[1536,1536]{1,0:T(8,128)(2,1)} %bitcast.23, f32[1,1536]{1,0:T(1,128)S(1)} %copy-done.4, ...), custom_call_target="tpu_custom_call" | custom-call | tf_op jit(solution)/shard_map/cross_and_compress/pallas_call | solution.py:337
  40.6 0.1 collective-permute-start.2
  40.7 1.2 %collective-permute-done.2.far_ref = bf16[128,64]{1,0:T(8,128)(2,1)S(1)} collective-permute-done((bf16[128,64]{1,0:T(8,128)(2,1)S(1)}, bf16[128,64]{1,0:T(8,128)(2,1)S(1)}, u32[]{:S(2)}, u32[]{:S(2)}) %collective-permute-start.2) | collective-permute-done | bytes 16416 | tf_op jit(solution)/shard_map/ppermute | solution.py:442
  41.9 2.1 %mix_experts.1 = bf16[128,4,256]{2,1,0:T(4,128)(2,1)} custom-call(s32[1]{0:T(128)} %bitcast.tower_ref, f32[8,128,256]{2,1,0:T(8,128)S(1)} %get-tuple-element.13.early_ref, bf16[8,128,256]{2,1,0:T(8,128)(2,1)S(1)} %get-tuple-element.14.late_ref, f32[128,32]{1,0:T(8,128)S(1)} %get-tuple-element.15.gate_early_ref, ...), custom_call_target="tpu_custom_call" | custom-call | tf_op jit(solution)/shard_map/mix_experts/pallas_call | solution.py:389
Async XLA Ops:
  0.0 24.7 %copy-start.3 = (f32[4,512]{1,0:T(4,128)S(1)}, f32[4,512]{1,0:T(4,128)}, u32[]{:S(2)}) copy-start(f32[4,512]{1,0:T(4,128)} %own_bias_ref.1) | copy-start | bytes 24580
  0.0 31.5 %collective-permute-start = (bf16[4,1024,512]{2,1,0:T(8,128)(2,1)}, bf16[4,1024,512]{2,1,0:T(8,128)(2,1)}, u32[]{:S(2)}, u32[]{:S(2)}) collective-permute-start(bf16[4,1024,512]{2,1,0:T(8,128)(2,1)} %own_hbm.1), channel_id=1, source_target_pairs={{0,8},{8,0},{1,9},{9,1},{2,10},{10,2},{3,11},{11,3},{4,12},{12,4},... | collective-permute-start | bytes 12582920 | tf_op jit(solution)/shard_map/ppermute | solution.py:422
  17.7 13.8 %copy-start = (bf16[128,896]{1,0:T(8,128)(2,1)S(1)}, bf16[128,896]{1,0:T(8,128)(2,1)}, u32[]{:S(2)}) copy-start(bf16[128,896]{1,0:T(8,128)(2,1)} %other_ref.1) | copy-start | bytes 688132
  17.7 13.8 %copy-start.2 = (bf16[1024,4,8]{0,2,1:T(8,128)(2,1)S(1)}, bf16[1024,4,8]{0,2,1:T(8,128)(2,1)}, u32[]{:S(2)}) copy-start(bf16[1024,4,8]{0,2,1:T(8,128)(2,1)} %param.23) | copy-start | bytes 196612
  17.7 19.4 %all-to-all-start = ((bf16[8,192,128]{2,1,0:T(8,128)(2,1)}), bf16[8,192,128]{2,1,0:T(8,128)(2,1)S(1)}, u32[]{:S(2)}, u32[]{:S(2)}) async-start(bf16[8,192,128]{2,1,0:T(8,128)(2,1)} %bitcast.24), calls=%async_computation | async-start | bytes 786432 | tf_op jit(solution)/shard_map/all_to_all | solution.py:430
  24.7 6.8 %collective-permute-start.1 = (f32[4,512]{1,0:T(4,128)S(1)}, f32[4,512]{1,0:T(4,128)S(1)}, u32[]{:S(2)}, u32[]{:S(2)}) collective-permute-start(f32[4,512]{1,0:T(4,128)S(1)} %copy-done.3), channel_id=1, source_target_pairs={{0,8},{8,0},{1,9},{9,1},{2,10},{10,2},{3,11},{11,3},{4,12},{12,4},... | collective-permute-start | bytes 24584 | tf_op jit(solution)/shard_map/ppermute | solution.py:423
  31.4 5.6 %copy-start.1 = (bf16[1,1536,64]{1,2,0:T(8,128)(2,1)S(1)}, bf16[1,1536,64]{1,2,0:T(8,128)(2,1)}, u32[]{:S(2)}) copy-start(bf16[1,1536,64]{1,2,0:T(8,128)(2,1)} %param.18) | copy-start | bytes 589828
  31.4 5.6 %copy-start.4 = (f32[1,1536]{1,0:T(1,128)S(1)}, f32[1,1536]{1,0:T(1,128)}, u32[]{:S(2)}) copy-start(f32[1,1536]{1,0:T(1,128)} %bias_ref.1) | copy-start | bytes 18436
  31.4 5.6 %copy-start.5 = (s32[1,64]{1,0:T(1,128)S(1)}, s32[1,64]{1,0:T(1,128)}, u32[]{:S(2)}) copy-start(s32[1,64]{1,0:T(1,128)} %param.14) | copy-start | bytes 772
  31.5 5.6 %copy-start.6 = (f32[1,64]{1,0:T(1,128)S(1)}, f32[1,64]{1,0:T(1,128)}, u32[]{:S(2)}) copy-start(f32[1,64]{1,0:T(1,128)} %comp_bias_ref.1) | copy-start | bytes 772
  40.6 1.3 %collective-permute-start.2 = (bf16[128,64]{1,0:T(8,128)(2,1)S(1)}, bf16[128,64]{1,0:T(8,128)(2,1)S(1)}, u32[]{:S(2)}, u32[]{:S(2)}) collective-permute-start(bf16[128,64]{1,0:T(8,128)(2,1)S(1)} %cross_and_compress.1.own_ref), channel_id=1, source_target_pairs={{0,8},{8,0},{1,9},{9,1},{2,10},{10,2},{3,11},{11,3},{4,12},{12,4},... | collective-permute-start | bytes 49160 | tf_op jit(solution)/shard_map/ppermute | solution.py:442

commit v6 on v5

--- a/solution.py
+++ b/solution.py
@@ -62,7 +62,8 @@
         for c in range(CHUNKS):
             where = (pl.ds(0, by_row), slice(None), pl.ds(c * width, width))
             parts.append(pltpu.make_async_copy(tab_hbm.at[where], tab.at[where], sem.at[3 + c]))
-            parts[-1].start()
+            if c < 2:
+                parts[-1].start()
     others = pl.ds(by_row, features - by_row)
     rest_copy = pltpu.make_async_copy(tab_hbm.at[others], tab.at[others], sem.at[2])
     if not by_row:
@@ -94,6 +95,8 @@
 
         for c in range(CHUNKS):
             parts[c].wait()
+            if c + 2 < CHUNKS:
+                parts[c + 2].start()
             if c == CHUNKS // 2 - 1:
                 rest_copy.start()
             lax.fori_loop(0, width // (2 * LOW), functools.partial(build, first=c * width), 0, unroll=8)

time: 44.2 us -> 44.5 us (level)
  no operation moved by 1% of the time
where the time goes in v6:
time: 44.5 us; the launch traced here: 44.2 us
  Pallas kernels  33 us (74%)
  starting transfers between devices  7.8 us (18%)
  waiting for transfers between devices  3.26 us (7%)
    pallas_call x1, Pallas kernels, pool_features(): pl.pallas_call(functools.partial(pool_kernel, by_row, tile, groups, row_c...  17.5 us
    all_to_all x1, starting transfers between devices, on_device(): lax.all_to_all(pooled, 'inner', split_axis=0, concat_axis=0, tiled=True)  7.01 us
    pallas_call x1, Pallas kernels, pool_own(): pl.pallas_call(own_kernel, out_shape=jax.ShapeDtypeStruct((features, embe...  6.41 us
    pallas_call x1, Pallas kernels, cross_and_compress(): pl.pallas_call(functools.partial(cross_kernel, each, by_row), out_shape=j...  3.52 us
    pallas_call x1, Pallas kernels, early_part(): pl.pallas_call(functools.partial(early_kernel, known), out_shape=(jax.Sha...  3.48 us
    pallas_call x1, Pallas kernels, mix_experts(): pl.pallas_call(mix_kernel, out_shape=jax.ShapeDtypeStruct((rows, tasks, c...  2.07 us
    all_to_all x1, waiting for transfers between devices, on_device(): lax.all_to_all(pooled, 'inner', split_axis=0, concat_axis=0, tiled=True)  2.06 us
    ppermute x1, waiting for transfers between devices, on_device(): opposite = lax.ppermute(squeezed, 'tower', swap)  1.19 us
  transfers between devices with their start and end apart: 4, of which 2 were waited for; matrix products, arithmetic and copies ran while one was open for 0% of the time, Pallas kernels for 62%

profile of v6, /device:TPU:0, one launch (start us, length us, event | category | flops | bytes accessed | tf_op | source)
XLA Modules:
  0.0 44.2 jit_solution(148891244348707774)
XLA Ops:
  0.0 0.0 copy-start.3
  0.0 0.5 %collective-permute-start = (bf16[4,1024,512]{2,1,0:T(8,128)(2,1)}, bf16[4,1024,512]{2,1,0:T(8,128)(2,1)}, u32[]{:S(2)}, u32[]{:S(2)}) collective-permute-start(bf16[4,1024,512]{2,1,0:T(8,128)(2,1)} %own_hbm.1), channel_id=1, source_target_pairs={{0,8},{8,0},{1,9},{9,1},{2,10},{10,2},{3,11},{11,3},{4,12},{12,4},... | collective-permute-start | bytes 12582920 | tf_op jit(solution)/shard_map/ppermute | solution.py:425
  0.5 17.5 %pool_features.1 = bf16[8,8,24,128]{3,2,1,0:T(8,128)(2,1)} custom-call(s32[1]{0:T(128)} %bitcast.1.refs_0_.me_ref, s32[8,4,1024]{2,1,0:T(4,128)} %bitcast.25, s32[8,1024]{1,0:T(8,128)} %bitcast.27, bf16[8,24,16384]{2,1,0:T(8,128)(2,1)} %bitcast.21), custom_call_target="tpu_custom_call" | custom-call | tf_op jit(solution)/shard_map/pool_features/pallas_call | solution.py:202
  17.9 0.0 copy-start
  18.0 0.0 copy-start.2
  18.0 7.0 %all-to-all-start = ((bf16[8,192,128]{2,1,0:T(8,128)(2,1)}), bf16[8,192,128]{2,1,0:T(8,128)(2,1)S(1)}, u32[]{:S(2)}, u32[]{:S(2)}) async-start(bf16[8,192,128]{2,1,0:T(8,128)(2,1)} %bitcast.24), calls=%async_computation | async-start | bytes 786432 | tf_op jit(solution)/shard_map/all_to_all | solution.py:433
  25.0 0.0 copy-done.3
  25.0 0.3 collective-permute-start.1
  25.2 6.4 %pool_own.1.own_ref = bf16[5,24,128]{2,1,0:T(8,128)(2,1)S(1)} custom-call(s32[1]{0:T(128)} %bitcast.1.refs_0_.me_ref, s32[8,4,1024]{2,1,0:T(4,128)} %bitcast.26, s32[8,1024]{1,0:T(8,128)} %bitcast.28, bf16[8,24,16384]{2,1,0:T(8,128)(2,1)} %bitcast.22), custom_call_target="tpu_custom_call" | custom-call | flops 2013265920 | bytes 6291456 | tf_op jit(solution)/shard_map/pool_own/pallas_call | solution.py:228
  31.7 0.0 copy-start.1
  31.7 0.0 copy-start.4
  31.7 0.0 copy-start.5
  31.7 0.0 copy-start.6
  31.7 0.0 collective-permute-done.1.far_bias_ref
  31.7 0.0 collective-permute-done.far_hbm
  31.7 0.0 copy-done
  31.7 0.0 copy-done.2
  31.8 3.5 %early_part.1 = (f32[8,128,256]{2,1,0:T(8,128)S(1)}, f32[128,32]{1,0:T(8,128)S(1)}, bf16[8,128,256]{2,1,0:T(8,128)(2,1)S(1)}, bf16[32,128]{1,0:T(8,128)(2,1)S(1)}) custom-call(s32[1]{0:T(128)} %bitcast.tower_ref, bf16[128,896]{1,0:T(8,128)(2,1)S(1)} %copy-done, bf16[4,1024,512]{2,1,0:T(8,128)(2,1)} %own_hbm.1, ...), custom_call_target="tpu_custom_call" | custom-call | flops 469762048 | bytes 4194304 | tf_op jit(solution)/shard_map/early_part/pallas_call | solution.py:284
  35.2 2.1 %all-to-all-done = bf16[8,192,128]{2,1,0:T(8,128)(2,1)S(1)} async-done(((bf16[8,192,128]{2,1,0:T(8,128)(2,1)}), bf16[8,192,128]{2,1,0:T(8,128)(2,1)S(1)}, u32[]{:S(2)}, u32[]{:S(2)}) %all-to-all-start) | async-done | bytes 393248 | tf_op jit(solution)/shard_map/all_to_all | solution.py:433
  37.3 0.0 copy-done.1
  37.3 0.0 copy-done.4
  37.3 0.0 copy-done.5
  37.3 0.0 copy-done.6
  37.3 3.5 %cross_and_compress.1.own_ref = bf16[128,64]{1,0:T(8,128)(2,1)S(1)} custom-call(s32[1]{0:T(128)} %bitcast.1.refs_0_.me_ref, s32[64]{0:T(128)S(1)} %bitcast.20, bf16[64,24,128]{2,1,0:T(8,128)(2,1)S(1)} %bitcast.17, bf16[5,24,128]{2,1,0:T(8,128)(2,1)S(1)} %pool_own.1.own_ref, bf16[1536,1536]{1,0:T(8,128)(2,1)} %bitcast.23, f32[1,1536]{1,0:T(1,128)S(1)} %copy-done.4, ...), custom_call_target="tpu_custom_call" | custom-call | tf_op jit(solution)/shard_map/cross_and_compress/pallas_call | solution.py:340
  40.8 0.1 collective-permute-start.2
  40.9 1.2 %collective-permute-done.2.far_ref = bf16[128,64]{1,0:T(8,128)(2,1)S(1)} collective-permute-done((bf16[128,64]{1,0:T(8,128)(2,1)S(1)}, bf16[128,64]{1,0:T(8,128)(2,1)S(1)}, u32[]{:S(2)}, u32[]{:S(2)}) %collective-permute-start.2) | collective-permute-done | bytes 16416 | tf_op jit(solution)/shard_map/ppermute | solution.py:445
  42.1 2.1 %mix_experts.1 = bf16[128,4,256]{2,1,0:T(4,128)(2,1)} custom-call(s32[1]{0:T(128)} %bitcast.tower_ref, f32[8,128,256]{2,1,0:T(8,128)S(1)} %get-tuple-element.13.early_ref, bf16[8,128,256]{2,1,0:T(8,128)(2,1)S(1)} %get-tuple-element.14.late_ref, f32[128,32]{1,0:T(8,128)S(1)} %get-tuple-element.15.gate_early_ref, ...), custom_call_target="tpu_custom_call" | custom-call | tf_op jit(solution)/shard_map/mix_experts/pallas_call | solution.py:392
Async XLA Ops:
  0.0 25.0 %copy-start.3 = (f32[4,512]{1,0:T(4,128)S(1)}, f32[4,512]{1,0:T(4,128)}, u32[]{:S(2)}) copy-start(f32[4,512]{1,0:T(4,128)} %own_bias_ref.1) | copy-start | bytes 24580
  0.0 31.7 %collective-permute-start = (bf16[4,1024,512]{2,1,0:T(8,128)(2,1)}, bf16[4,1024,512]{2,1,0:T(8,128)(2,1)}, u32[]{:S(2)}, u32[]{:S(2)}) collective-permute-start(bf16[4,1024,512]{2,1,0:T(8,128)(2,1)} %own_hbm.1), channel_id=1, source_target_pairs={{0,8},{8,0},{1,9},{9,1},{2,10},{10,2},{3,11},{11,3},{4,12},{12,4},... | collective-permute-start | bytes 12582920 | tf_op jit(solution)/shard_map/ppermute | solution.py:425
  17.9 13.8 %copy-start = (bf16[128,896]{1,0:T(8,128)(2,1)S(1)}, bf16[128,896]{1,0:T(8,128)(2,1)}, u32[]{:S(2)}) copy-start(bf16[128,896]{1,0:T(8,128)(2,1)} %other_ref.1) | copy-start | bytes 688132
  18.0 13.8 %copy-start.2 = (bf16[1024,4,8]{0,2,1:T(8,128)(2,1)S(1)}, bf16[1024,4,8]{0,2,1:T(8,128)(2,1)}, u32[]{:S(2)}) copy-start(bf16[1024,4,8]{0,2,1:T(8,128)(2,1)} %param.23) | copy-start | bytes 196612
  18.0 19.3 %all-to-all-start = ((bf16[8,192,128]{2,1,0:T(8,128)(2,1)}), bf16[8,192,128]{2,1,0:T(8,128)(2,1)S(1)}, u32[]{:S(2)}, u32[]{:S(2)}) async-start(bf16[8,192,128]{2,1,0:T(8,128)(2,1)} %bitcast.24), calls=%async_computation | async-start | bytes 786432 | tf_op jit(solution)/shard_map/all_to_all | solution.py:433
  25.0 6.7 %collective-permute-start.1 = (f32[4,512]{1,0:T(4,128)S(1)}, f32[4,512]{1,0:T(4,128)S(1)}, u32[]{:S(2)}, u32[]{:S(2)}) collective-permute-start(f32[4,512]{1,0:T(4,128)S(1)} %copy-done.3), channel_id=1, source_target_pairs={{0,8},{8,0},{1,9},{9,1},{2,10},{10,2},{3,11},{11,3},{4,12},{12,4},... | collective-permute-start | bytes 24584 | tf_op jit(solution)/shard_map/ppermute | solution.py:426
  31.7 5.6 %copy-start.1 = (bf16[1,1536,64]{1,2,0:T(8,128)(2,1)S(1)}, bf16[1,1536,64]{1,2,0:T(8,128)(2,1)}, u32[]{:S(2)}) copy-start(bf16[1,1536,64]{1,2,0:T(8,128)(2,1)} %param.18) | copy-start | bytes 589828
  31.7 5.6 %copy-start.4 = (f32[1,1536]{1,0:T(1,128)S(1)}, f32[1,1536]{1,0:T(1,128)}, u32[]{:S(2)}) copy-start(f32[1,1536]{1,0:T(1,128)} %bias_ref.1) | copy-start | bytes 18436
  31.7 5.6 %copy-start.5 = (s32[1,64]{1,0:T(1,128)S(1)}, s32[1,64]{1,0:T(1,128)}, u32[]{:S(2)}) copy-start(s32[1,64]{1,0:T(1,128)} %param.14) | copy-start | bytes 772
  31.7 5.6 %copy-start.6 = (f32[1,64]{1,0:T(1,128)S(1)}, f32[1,64]{1,0:T(1,128)}, u32[]{:S(2)}) copy-start(f32[1,64]{1,0:T(1,128)} %comp_bias_ref.1) | copy-start | bytes 772
  40.8 1.3 %collective-permute-start.2 = (bf16[128,64]{1,0:T(8,128)(2,1)S(1)}, bf16[128,64]{1,0:T(8,128)(2,1)S(1)}, u32[]{:S(2)}, u32[]{:S(2)}) collective-permute-start(bf16[128,64]{1,0:T(8,128)(2,1)S(1)} %cross_and_compress.1.own_ref), channel_id=1, source_target_pairs={{0,8},{8,0},{1,9},{9,1},{2,10},{10,2},{3,11},{11,3},{4,12},{12,4},... | collective-permute-start | bytes 49160 | tf_op jit(solution)/shard_map/ppermute | solution.py:445
